TPU v7x, 32 devices: a whole 2x2x4 slice. The times are simulated.
32 devices in a mesh: wide: 8 (over z, x), narrow: 4 (over y, core).
Axes of the slice: x: 2, y: 2, z: 4, core: 2. Of those that a mesh axis runs over, the one named last changes fastest.
Arguments:
- coefficients: bfloat16 [512, 2, 512], P(('wide', 'narrow')), may hold values from -6 to 6
- radiation: bfloat16 [2, 512, 882], replicated, may hold values from -0.1875 to 0.1875
- interpolation: bfloat16 [882, 3328], replicated, may hold values from -0.21875 to 0.21875
- angles: float32 [8, 3328], replicated, may hold values from -3.140625 to 3.140625
- translations: float32 [316, 2, 3328], P(None, None, 'wide'), may hold values from -0.031746034 to 0.031746034
- sources: int32 [64, 189], P(('wide', 'narrow')), may hold values from 0 to 63
- operators: int32 [64, 189], P(('wide', 'narrow')), may hold values from 0 to 315
- counts: int32 [64], P(('wide', 'narrow')), may hold values from 63 to 189, as said below
Outputs:
- product: float32 [512, 2, 512], P(('wide', 'narrow'))
Inputs may be any that keep to these rules, and one draw needn't show every extreme that they name: `counts`: entries of a list past its count are not used; some parent has exactly 189 entries and some exactly 63. `sources`: index values; a program may hold and send them packed several to one 32-bit word, as an allowed encoding. `operators`: index values; a program may hold and send them packed several to one 32-bit word, as an allowed encoding.
All inputs are finite; a program needn't handle non-finite values.
Results may differ from a plain program's by a relative error of at most 0.005.
Values sent between devices are 32-bit elements; how exact they have to be, the bound alone decides.
No kernel may reach another device: no remote copies, remote signals or barrier semaphores. Data moves between devices by JAX's collectives and lax.ppermute only.
A program may use at most 128 MiB of HBM per device.

v0:
```python
import jax
import jax.numpy as jnp
from jax import lax
from jax.sharding import PartitionSpec as P


def product_of(left, right):
    return jnp.dot(left, right, preferred_element_type=jnp.float32)


def translate(patterns, operator_table, source_index, operator_index, weights):
    pat_real = patterns[:, 0]
    pat_imag = patterns[:, 1]
    tab_real = operator_table[:, 0]
    tab_imag = operator_table[:, 1]
    pick_real = jnp.take(pat_real, source_index, axis=0)
    pick_imag = jnp.take(pat_imag, source_index, axis=0)
    oper_real = jnp.take(tab_real, operator_index, axis=0)
    oper_imag = jnp.take(tab_imag, operator_index, axis=0)
    weight = weights[:, :, None]
    total_real = jnp.sum(weight * (oper_real * pick_real - oper_imag * pick_imag), 1)
    total_imag = jnp.sum(weight * (oper_real * pick_imag + oper_imag * pick_real), 1)
    return jnp.stack([total_real, total_imag], 1)


def on_device(
    coefficients, radiation, interpolation, angles, translations, sources, operators, counts
):
    box_dev = coefficients.shape[0]
    parents_dev = box_dev // 8
    leaf_dirs = interpolation.shape[0]
    parent_dirs = interpolation.shape[1]
    n_wide = lax.axis_size("wide")
    n_narrow = lax.axis_size("narrow")
    coef_real = coefficients[:, 0]
    coef_imag = coefficients[:, 1]
    rad_real = radiation[0]
    rad_imag = radiation[1]
    leaf_real = product_of(coef_real, rad_real) - product_of(coef_imag, rad_imag)
    leaf_imag = product_of(coef_real, rad_imag) + product_of(coef_imag, rad_real)
    leaf = jnp.stack([leaf_real, leaf_imag], 1).astype(jnp.bfloat16)
    upward = product_of(leaf.reshape(box_dev * 2, leaf_dirs), interpolation).reshape(
        parents_dev, 8, 2, parent_dirs
    )
    cosines = jnp.cos(angles)[None]
    sines = jnp.sin(angles)[None]
    out_real = jnp.sum(cosines * upward[:, :, 0] - sines * upward[:, :, 1], 1)
    out_imag = jnp.sum(cosines * upward[:, :, 1] + sines * upward[:, :, 0], 1)
    outgoing = jnp.stack([out_real, out_imag], 1)
    list_ids, list_ops, list_lens = (
        lax.all_gather(sources, "wide", axis=0, tiled=True),
        lax.all_gather(operators, "wide", axis=0, tiled=True),
        lax.all_gather(counts, "wide", axis=0, tiled=True),
    )
    positions = jnp.arange(list_ids.shape[1], dtype=jnp.int32)
    weights = (positions[None, :] < list_lens[:, None]).astype(jnp.float32)
    own_slice = lax.all_to_all(outgoing, "wide", split_axis=2, concat_axis=0, tiled=True)
    every = lax.all_gather(own_slice, "narrow", axis=0, tiled=True)
    owner = list_ids // parents_dev
    local_ids = (
        owner % n_narrow * n_wide + owner // n_narrow
    ) * parents_dev + list_ids % parents_dev
    incoming = translate(every, translations, local_ids, list_ops, weights)
    back = lax.all_to_all(incoming, "wide", split_axis=0, concat_axis=2, tiled=True)
    in_real = back[:, 0]
    in_imag = back[:, 1]
    down_real = cosines * in_real[:, None] + sines * in_imag[:, None]
    down_imag = cosines * in_imag[:, None] - sines * in_real[:, None]
    downward = jnp.stack([down_real, down_imag], 2).astype(jnp.bfloat16)
    received = lax.dot_general(
        downward.reshape(box_dev * 2, parent_dirs),
        interpolation,
        (((1,), (1,)), ((), ())),
        preferred_element_type=jnp.float32,
    )
    received = received.astype(jnp.bfloat16).reshape(box_dev, 2, leaf_dirs)
    dims = (((1,), (1,)), ((), ()))
    recv_real = received[:, 0]
    recv_imag = received[:, 1]
    res_real = lax.dot_general(
        recv_real, rad_real, dims, preferred_element_type=jnp.float32
    ) + lax.dot_general(recv_imag, rad_imag, dims, preferred_element_type=jnp.float32)
    res_imag = lax.dot_general(
        recv_imag, rad_real, dims, preferred_element_type=jnp.float32
    ) - lax.dot_general(recv_real, rad_imag, dims, preferred_element_type=jnp.float32)
    return jnp.stack([res_real, res_imag], 1)


def solution(mesh):
    in_specs = (
        P(("wide", "narrow"), None, None),
        P(),
        P(),
        P(),
        P(None, None, "wide"),
        P(("wide", "narrow"), None),
        P(("wide", "narrow"), None),
        P(("wide", "narrow")),
    )
    out_specs = P(("wide", "narrow"), None, None)
    return jax.shard_map(
        on_device, mesh=mesh, in_specs=in_specs, out_specs=out_specs, check_vma=False
    )
```

profile of v0, /device:TPU:0, one launch (start us, length us, event | category | flops | bytes accessed | tf_op | source)
XLA Modules:
  0.0 247.8 jit_solution(5747227957491423294)
XLA Ops:
  0.0 5.3 %fusion.27 = (bf16[1,512,882]{1,0,2:T(2,128)(2,1)S(1)}, bf16[1,512,882]{1,0,2:T(2,128)(2,1)S(1)}) fusion(bf16[2,512,882]{1,0,2:T(2,128)(2,1)} %param.13), kind=kLoop, calls=%fused_computation.77 | loop fusion | bytes 3612672 | tf_op jit(solution)/shard_map/slice | solution.py:38
  5.4 0.5 copy_bitcast_fusion
  5.9 0.3 fusion.25
  6.2 0.4 fusion.24
  6.6 0.4 fusion.7
  6.9 0.4 fusion.6
  7.3 0.4 fusion.29
  7.7 0.9 fusion
  8.7 0.2 subtract_reduce_fusion
  8.9 3.5 %copy.123 = f32[2,2,3328]{1,0,2:T(2,128)} copy(f32[2,2,3328]{2,0,1:T(2,128)S(1)} %pad_maximum_fusion.3) | data formatting | bytes 106496 | tf_op jit(solution)/shard_map/stack | solution.py:49
  12.4 5.8 %reshape.140 = f32[8,1,1664]{2,1,0:T(1,128)} reshape(f32[3328,2,2]{2,1,0:T(2,128)} %bitcast.95) | data formatting | bytes 106496
  18.3 7.3 %all-to-all-start = ((f32[8,1,1664]{2,1,0:T(1,128)}), f32[8,1,1664]{2,1,0:T(1,128)S(1)}, u32[]{:S(2)}, u32[]{:S(2)}) async-start(f32[8,1,1664]{2,1,0:T(1,128)} %reshape.140), calls=%async_computation | async-start | bytes 106496 | tf_op jit(solution)/shard_map/all_to_all | solution.py:57
  25.5 26.5 %all-gather = s32[8,2,189]{2,1,0:T(2,128)S(1)} all-gather(s32[1,2,189]{2,1,0:T(2,128)S(1)} %bitcast.105), channel_id=1, replica_groups=mesh['wide'=8,'narrow'=4] {'wide'}, dimensions={0}, use_global_device_ids=true | all-gather | bytes 13608 | tf_op jit(solution)/shard_map/all_gather | solution.py:52
  52.1 26.2 %all-gather.1 = s32[8,2,189]{2,1,0:T(2,128)S(1)} all-gather(s32[1,2,189]{2,1,0:T(2,128)S(1)} %bitcast.106), channel_id=1, replica_groups=mesh['wide'=8,'narrow'=4] {'wide'}, dimensions={0}, use_global_device_ids=true | all-gather | bytes 13608 | tf_op jit(solution)/shard_map/all_gather | solution.py:51
  78.6 2.2 fusion.28
  80.8 1.3 copy.143
  82.1 12.8 %gather_fusion = f32[3024,416]{1,0:T(8,128)} fusion(f32[316,416]{1,0:T(8,128)S(1)} %bitcast.92, s32[3072]{0:T(1024)S(1)} %pad_clamp_fusion.1), kind=kCustom, calls=%fused_computation.clone | custom fusion | bytes 10075968 | tf_op jit(solution)/shard_map/jit(_take)/gather | solution.py:18
  94.9 4.9 %reshape.136 = f32[16,189,416]{2,1,0:T(8,128)} reshape(f32[3024,416]{1,0:T(8,128)} %gather_fusion) | data formatting | bytes 10063872 | tf_op jit(solution)/shard_map/jit(_take)/gather | solution.py:18
  99.8 9.2 %copy.136 = f32[16,189,416]{1,0,2:T(8,128)} copy(f32[16,189,416]{2,1,0:T(8,128)} %reshape.136) | data formatting | bytes 10063872 | tf_op jit(solution)/shard_map/jit(_take)/gather | solution.py:18
  109.1 0.2 copy.149
  109.3 12.9 %gather_fusion.2 = f32[3024,416]{1,0:T(8,128)} fusion(f32[316,416]{1,0:T(8,128)S(1)} %bitcast.91, s32[3072]{0:T(1024)S(1)} %pad_clamp_fusion.1), kind=kCustom, calls=%fused_computation.2.clone | custom fusion | bytes 10075968 | tf_op jit(solution)/shard_map/jit(_take)/gather | solution.py:19
  122.2 4.9 %reshape.138 = f32[16,189,416]{2,1,0:T(8,128)} reshape(f32[3024,416]{1,0:T(8,128)} %gather_fusion.2) | data formatting | bytes 10063872 | tf_op jit(solution)/shard_map/jit(_take)/gather | solution.py:19
  127.1 0.6 dynamic-slice
  128.3 0.2 dynamic-update-slice
  128.6 9.2 %copy.139 = f32[16,189,416]{1,0,2:T(8,128)} copy(f32[16,189,416]{2,1,0:T(8,128)} %reshape.138) | data formatting | bytes 10063872 | tf_op jit(solution)/shard_map/jit(_take)/gather | solution.py:19
  137.7 7.8 %all-reduce = s32[16]{0:T(128)S(1)} all-reduce(s32[16]{0:T(128)S(1)} %dynamic-update-slice), channel_id=1, replica_groups=mesh['wide'=8,'narrow'=4] {'wide'}, use_global_device_ids=true, to_apply=%add | all-reduce | flops 16 | bytes 128
  145.6 0.5 broadcast.111
  146.1 0.8 reduce
  146.9 6.8 %reshape.141 = f32[3328,2,2]{2,1,0:T(2,128)} reshape(f32[8,1664]{1,0:T(8,128)S(1)} %reduce) | data formatting | bytes 106496
  153.8 3.5 %copy.137 = f32[2,2,8,416]{3,2,1,0:T(8,128)S(1)} copy(f32[2,2,8,416]{1,0,3,2:T(2,128)} %bitcast.96) | data formatting | bytes 106496 | tf_op jit(solution)/shard_map/all_to_all | solution.py:57
  157.3 5.8 %all_gather.14 = f32[64,2,416]{2,0,1:T(8,128)S(1)} all-gather(f32[16,2,416]{2,0,1:T(8,128)S(1)} %all_to_all.29), channel_id=1, replica_groups=mesh['wide'=8,'narrow'=4] {'narrow'}, dimensions={0}, use_global_device_ids=true | all-gather | bytes 266240 | tf_op jit(solution)/shard_map/all_gather | solution.py:58
  163.1 12.8 %gather_fusion.1 = f32[3024,416]{1,0:T(8,128)} fusion(f32[64,416]{1,0:T(8,128)S(1)} %get-tuple-element.19, s32[3072]{0:T(1024)S(1)} %pad_clamp_fusion), kind=kCustom, calls=%fused_computation.1.clone | custom fusion | bytes 10075968 | tf_op jit(solution)/shard_map/jit(_take)/gather | solution.py:16
  175.9 4.9 %reshape.137 = f32[16,189,416]{2,1,0:T(8,128)} reshape(f32[3024,416]{1,0:T(8,128)} %gather_fusion.1) | data formatting | bytes 10063872 | tf_op jit(solution)/shard_map/jit(_take)/gather | solution.py:16
  180.9 9.2 %copy.138 = f32[16,189,416]{1,0,2:T(8,128)} copy(f32[16,189,416]{2,1,0:T(8,128)} %reshape.137) | data formatting | bytes 10063872 | tf_op jit(solution)/shard_map/jit(_take)/gather | solution.py:16
  190.1 12.9 %gather_fusion.3 = f32[3024,416]{1,0:T(8,128)} fusion(f32[64,416]{1,0:T(8,128)S(1)} %get-tuple-element.20, s32[3072]{0:T(1024)S(1)} %pad_clamp_fusion), kind=kCustom, calls=%fused_computation.3.clone | custom fusion | bytes 10075968 | tf_op jit(solution)/shard_map/jit(_take)/gather | solution.py:17
  202.9 4.9 %reshape.139 = f32[16,189,416]{2,1,0:T(8,128)} reshape(f32[3024,416]{1,0:T(8,128)} %gather_fusion.3) | data formatting | bytes 10063872 | tf_op jit(solution)/shard_map/jit(_take)/gather | solution.py:17
  207.8 9.2 %copy.140 = f32[16,189,416]{1,0,2:T(8,128)} copy(f32[16,189,416]{2,1,0:T(8,128)} %reshape.139) | data formatting | bytes 10063872 | tf_op jit(solution)/shard_map/jit(_take)/gather | solution.py:17
  217.0 11.0 %multiply_reduce_fusion.1 = (f32[16,416]{0,1:T(8,128)S(1)}, f32[16,416]{0,1:T(8,128)S(1)}) fusion(f32[16,189,416]{1,0,2:T(8,128)} %copy.140, f32[16,189,416]{1,0,2:T(8,128)} %copy.139, f32[16,189,416]{1,0,2:T(8,128)} %copy.138, f32[16,189,416]{1,0,2:T(8,128)} %copy.136, f32[16,189]{1,0:T(8,128)S(1)} %fusion.17, pred[16,189]{1,0:T(8,128)(4,1)S(1)} %get-tuple-element.11, ...), kind=kLoop, calls=%fused_computation.5 | loop fusion | flops 17598464 | bytes 20199136 | tf_op jit(solution)/shard_map/reduce_sum | solution.py:21
  228.0 0.2 copy.130
  228.2 12.0 %all_to_all.36 = f32[16,2,416]{2,1,0:T(2,128)S(1)} all-to-all(f32[16,2,416]{2,1,0:T(2,128)S(1)} %copy.130), channel_id=1, replica_groups=mesh['wide'=8,'narrow'=4] {'wide'}, dimensions={0} | all-to-all | bytes 106496 | tf_op jit(solution)/shard_map/all_to_all | solution.py:64
  240.5 0.4 add_convert_fusion
  240.9 0.5 pad_maximum_fusion.1
  241.5 4.5 %convolution_convert_fusion = bf16[32,882]{1,0:T(8,128)(2,1)S(1)} fusion(bf16[32,3328]{1,0:T(8,128)(2,1)S(1)} %convert_element_type.19, bf16[882,3328]{1,0:T(8,128)(2,1)} %param.14), kind=kOutput, calls=%fused_computation.8 | convolution fusion | flops 187887168 | bytes 6140032 | tf_op jit(solution)/shard_map/dot_general | solution.py:70
  246.1 0.2 fusion.22
  246.4 0.2 fusion.23
  246.6 0.2 fusion.5
  246.8 0.2 fusion.4
  247.1 0.7 copy.134
  (44 shorter events, 1.1 us)
Async XLA Ops:
  0.0 5.3 %copy-start = (bf16[16,2,512]{2,1,0:T(2,128)(2,1)S(1)}, bf16[16,2,512]{2,1,0:T(2,128)(2,1)}, u32[]{:S(2)}) copy-start(bf16[16,2,512]{2,1,0:T(2,128)(2,1)} %param.12) | copy-start | bytes 98308
  0.0 7.7 %slice-start = ((s8[5910528]{0:T(1024)(128)(4,1)}), s8[1716224]{0:T(1024)(128)(4,1)S(1)}, s32[]{:S(2)}) async-start(s8[5910528]{0:T(1024)(128)(4,1)} %bitcast.93), calls=%async_computation.2 | async-start | bytes 3432448
  5.3 2.0 copy-start.1
  5.3 2.4 slice-start.1
  7.7 17.8 %copy-start.2 = (s32[2,189]{1,0:T(2,128)S(1)}, s32[2,189]{1,0:T(2,128)}, u32[]{:S(2)}) copy-start(s32[2,189]{1,0:T(2,128)} %param.18) | copy-start | bytes 4540
  7.7 44.4 %copy-start.3 = (s32[2,189]{1,0:T(2,128)S(1)}, s32[2,189]{1,0:T(2,128)}, u32[]{:S(2)}) copy-start(s32[2,189]{1,0:T(2,128)} %param.17) | copy-start | bytes 4540
  18.3 127.3 %all-to-all-start = ((f32[8,1,1664]{2,1,0:T(1,128)}), f32[8,1,1664]{2,1,0:T(1,128)S(1)}, u32[]{:S(2)}, u32[]{:S(2)}) async-start(f32[8,1,1664]{2,1,0:T(1,128)} %reshape.140), calls=%async_computation | async-start | bytes 106496 | tf_op jit(solution)/shard_map/all_to_all | solution.py:57
  122.2 4.9 %copy-start.5 = (u32[32]{0:T(128)S(1)}, u32[32]{0:T(128)}, u32[]{:S(2)}) copy-start(u32[32]{0:T(128)} %constant.76) | copy-start | bytes 388
  122.2 6.2 %copy-start.4 = (s32[2]{0:T(128)S(1)}, s32[2]{0:T(128)}, u32[]{:S(2)}) copy-start(s32[2]{0:T(128)} %param.19) | copy-start | bytes 28
where the time goes:
time: 249 us; the launch traced here: 248 us
  local copies, waits for them, and re-layouts  140 us (56%)
  blocking collectives  78.3 us (31%)
  other arithmetic  13.1 us (5%)
  matrix products  7.72 us (3%)
  starting transfers between devices  7.25 us (3%)
    gather x3, local copies, waits for them, and re-layouts, translate(): oper_real = jnp.take(tab_real, operator_index, axis=0)  26.9 us
    gather x3, local copies, waits for them, and re-layouts, translate(): pick_real = jnp.take(pat_real, source_index, axis=0)  26.9 us
    gather x3, local copies, waits for them, and re-layouts, translate(): pick_imag = jnp.take(pat_imag, source_index, axis=0)  26.9 us
    gather x3, local copies, waits for them, and re-layouts, translate(): oper_imag = jnp.take(tab_imag, operator_index, axis=0)  26.9 us
    all_gather x1, blocking collectives, on_device(): lax.all_gather(operators, 'wide', axis=0, tiled=True)  26.5 us
    all_gather x1, blocking collectives, on_device(): lax.all_gather(sources, 'wide', axis=0, tiled=True)  26.2 us
    unnamed x27, local copies, waits for them, and re-layouts  15.2 us
    all_to_all x1, blocking collectives, on_device(): lax.all_to_all(incoming, 'wide', split_axis=0, concat_axis=2, tiled=True)  12 us
  transfers between devices with their start and end apart: 1, of which 0 were waited for; matrix products, arithmetic and copies ran while one was open for 24% of the time, Pallas kernels for 0%

commit v1 on v0

v1 whole, which is shorter than its diff:
```python
import jax
import jax.numpy as jnp
from jax import lax
from jax.experimental import pallas as pl
from jax.experimental.pallas import tpu as pltpu
from jax.sharding import PartitionSpec as P

F32 = jnp.float32
BF16 = jnp.bfloat16
MIB = 2**20
NT = (((1,), (1,)), ((), ()))


class Plan:
    def __init__(self, parents, dirs, length, ops):
        self.parents = parents
        self.dirs = dirs
        self.length = length
        self.ops = ops
        self.tiles = -(-dirs // 128)
        self.width = 128 * self.tiles
        spare = self.width - dirs
        used = dirs - 128 * (self.tiles - 1)
        self.bits = (ops - 1).bit_length()
        if 2 * spare >= length:
            self.extra = 0
            self.pieces = [
                (self.tiles - 1, used, spare, 0),
                (2 * self.tiles - 1, used, length - spare, spare),
            ]
        else:
            self.extra = -(-length // 128)
            self.pieces = [
                (2 * self.tiles + e, 0, min(128, length - 128 * e), 128 * e)
                for e in range(self.extra)
            ]
        self.rows = 2 * self.tiles + self.extra
        self.code_width = -(-length // 128) * 128


def sin_cos(angle):
    turns = jnp.floor(angle * 0.6366197723675814 + 0.5)
    quarter = turns.astype(jnp.int32)
    rest = angle - turns * 1.5703125
    rest = rest - turns * 4.837512969970703e-4
    rest = rest - turns * 7.54978995489188e-8
    square = rest * rest
    sine = ((-1.9515295891e-4 * square + 8.3321608736e-3) * square - 1.6666654611e-1) * square * rest + rest
    cosine = ((2.443315711809948e-5 * square - 1.388731625493765e-3) * square + 4.166664568298827e-2) * (
        square * square
    ) - 0.5 * square + 1.0
    swap = (quarter & 1) == 1
    sin_value = jnp.where(swap, cosine, sine)
    cos_value = jnp.where(swap, sine, cosine)
    sin_value = jnp.where((quarter & 2) == 2, -sin_value, sin_value)
    cos_value = jnp.where(((quarter + 1) & 2) == 2, -cos_value, cos_value)
    return sin_value, cos_value


def arrange(boxes, swapped):
    row = lax.broadcasted_iota(jnp.int32, (128, 2 * boxes), 0)
    column = lax.broadcasted_iota(jnp.int32, (128, 2 * boxes), 1)
    real_at = 2 * row
    imag_at = 2 * (row - boxes) + 1
    if swapped:
        first = jnp.where((row < boxes) & (column == real_at + 1), -1.0, 0.0)
        second = jnp.where((row >= boxes) & (row < 2 * boxes) & (column == imag_at - 1), 1.0, 0.0)
    else:
        first = jnp.where((row < boxes) & (column == real_at), 1.0, 0.0)
        second = jnp.where((row >= boxes) & (row < 2 * boxes) & (column == imag_at), 1.0, 0.0)
    return (first + second).astype(BF16)


def upward_kernel(plan, n_wide, n_narrow, chunk):
    def kernel(
        counts, coef, rad_hbm, interp_hbm, angles, sources, operators,
        send, cos_out, sin_out,
        rad, interp, even, odd, codes, real_buf, imag_buf, sems,
    ):
        parent_dirs = angles.shape[1]
        leaf_dirs = rad.shape[0]
        boxes = coef.shape[0]
        parents_dev = boxes // 8
        n_chunks = parent_dirs // chunk
        rad_copy = pltpu.make_async_copy(rad_hbm, rad, sems.at[n_chunks])
        rad_copy.start()
        copies = []
        for c in range(n_chunks):
            cut = (slice(None), pl.ds(c * chunk, chunk))
            copies.append(pltpu.make_async_copy(interp_hbm.at[cut], interp.at[cut], sems.at[c]))
            copies[-1].start()

        sines, cosines = sin_cos(angles[...])
        sin_out[...] = sines
        cos_out[...] = cosines

        code = sources[...] * (1 << plan.bits) + operators[...]
        at = lax.broadcasted_iota(jnp.int32, code.shape, 1)
        parent = lax.broadcasted_iota(jnp.int32, code.shape, 0)
        limit = jnp.zeros(code.shape, jnp.int32)
        for p in range(parents_dev):
            limit = jnp.where(parent == p, counts[p], limit)
        codes[...] = jnp.full(codes.shape, -1.0, F32)
        codes[:, 0 : plan.length] = jnp.where(at < limit, code, -1).astype(F32)

        rows = coef[...].reshape(2 * boxes, coef.shape[2])
        plain = jnp.dot(arrange(boxes, False), rows, preferred_element_type=F32).astype(BF16)
        turned = jnp.dot(arrange(boxes, True), rows, preferred_element_type=F32).astype(BF16)
        weights = jnp.concatenate([plain, turned], 0)

        rad_copy.wait()
        matrix = rad[...].reshape(2 * leaf_dirs, rad.shape[2])
        both = lax.dot_general(matrix, weights, NT, preferred_element_type=F32)
        even[...] = both[:, 0:128]
        odd[...] = both[:, 128:256]
        leaf_t = even[pl.ds(0, leaf_dirs, stride=2), :] + odd[pl.ds(1, leaf_dirs, stride=2), :]
        leaf = jnp.transpose(leaf_t)[0 : 2 * boxes].astype(BF16)

        for c in range(n_chunks):
            copies[c].wait()
            cut = slice(c * chunk, (c + 1) * chunk)
            up = jnp.dot(leaf, interp[:, cut], preferred_element_type=F32)
            cs = cos_out[:, cut]
            sn = sin_out[:, cut]
            for p in range(parents_dev):
                up_real = up[8 * p : 8 * p + 8]
                up_imag = up[boxes + 8 * p : boxes + 8 * p + 8]
                real_buf[p : p + 1, cut] = jnp.sum(cs * up_real - sn * up_imag, 0, keepdims=True)
                imag_buf[p : p + 1, cut] = jnp.sum(cs * up_imag + sn * up_real, 0, keepdims=True)

        lane = lax.broadcasted_iota(jnp.int32, (parents_dev, 128), 1)
        tails = {}
        for tile, start, count, first in plan.pieces:
            turn = (start - first) % plan.code_width
            moved = codes[...] if turn == 0 else pltpu.roll(codes[...], turn, 1)
            tails[tile] = (moved[:, 0:128], (lane >= start) & (lane < start + count))
        for w in range(n_wide):
            base = plan.dirs * w // 128 * 128
            shift = plan.dirs * w % 128
            span = -(-(shift + plan.dirs) // 128) * 128
            span = min(max(span, plan.width), parent_dirs - base)
            for part, buf in ((0, real_buf), (1, imag_buf)):
                value = buf[:, base : base + span]
                if shift:
                    value = pltpu.roll(value, span - shift, 1)
                for k in range(plan.tiles):
                    tile = part * plan.tiles + k
                    piece = value[:, 128 * k : 128 * k + 128]
                    if k == plan.tiles - 1:
                        piece = jnp.where(lane < plan.dirs - 128 * k, piece, -1.0)
                    if tile in tails:
                        piece = jnp.where(tails[tile][1], tails[tile][0], piece)
                    for n in range(n_narrow):
                        first = (w * n_narrow + n) * parents_dev * plan.rows + tile
                        send[pl.ds(first, parents_dev, stride=plan.rows), :] = piece
            for e in range(plan.extra):
                tile = 2 * plan.tiles + e
                piece = jnp.where(tails[tile][1], tails[tile][0], -1.0)
                for n in range(n_narrow):
                    first = (w * n_narrow + n) * parents_dev * plan.rows + tile
                    send[pl.ds(first, parents_dev, stride=plan.rows), :] = piece

    return kernel


def translate_kernel(plan, n_wide, n_narrow, parents_dev):
    targets = n_wide * parents_dev
    group = max(1, min(targets, 1024 // plan.parents))
    step = min(256, plan.width)

    def kernel(table_in, received, out, table, tally, a_real, a_imag):
        mine = lax.axis_index("narrow")
        table[...] = jnp.zeros(table.shape, BF16)
        table[:, 0 : plan.dirs, 0 : plan.ops] = table_in[...].astype(BF16)
        lane = lax.broadcasted_iota(jnp.int32, (1, 128), 1)
        source_at = lax.broadcasted_iota(jnp.int32, (plan.parents, 128), 0)
        op_at = lax.broadcasted_iota(jnp.int32, (table.shape[2], 128), 0)

        def do_group(first_target):
            for i in range(group):
                target = first_target + i
                w = target // parents_dev
                p = target % parents_dev
                row = ((w * n_narrow + mine) * parents_dev + p) * plan.rows
                hits, picks = [], []
                for tile, start, count, _ in plan.pieces:
                    code = received[pl.ds(row + tile, 1), :]
                    code = jnp.where((lane >= start) & (lane < start + count), code, -1.0).astype(jnp.int32)
                    hits.append(jnp.where(source_at == (code >> plan.bits), 1.0, 0.0).astype(BF16))
                    picks.append(jnp.where(op_at == (code & ((1 << plan.bits) - 1)), 1.0, 0.0).astype(BF16))
                count_of = lax.dot_general(
                    jnp.concatenate(hits, 1), jnp.concatenate(picks, 1), NT, preferred_element_type=F32
                )
                tally[i * plan.parents : (i + 1) * plan.parents, :] = count_of.astype(BF16)
            for j in range(plan.width // step):
                cut = slice(j * step, (j + 1) * step)
                a_real[...] = lax.dot_general(tally[...], table[0, cut, :], NT, preferred_element_type=F32)
                a_imag[...] = lax.dot_general(tally[...], table[1, cut, :], NT, preferred_element_type=F32)
                for q in range(step // 128):
                    k = j * (step // 128) + q
                    lanes = slice(128 * q, 128 * q + 128)
                    out_real = received[pl.ds(k, plan.parents, stride=plan.rows), :]
                    out_imag = received[pl.ds(plan.tiles + k, plan.parents, stride=plan.rows), :]
                    for i in range(group):
                        own = slice(i * plan.parents, (i + 1) * plan.parents)
                        op_real = a_real[own, lanes]
                        op_imag = a_imag[own, lanes]
                        real = jnp.sum(op_real * out_real - op_imag * out_imag, 0, keepdims=True)
                        imag = jnp.sum(op_real * out_imag + op_imag * out_real, 0, keepdims=True)
                        at = (first_target + i) * 2 * plan.tiles + k
                        out[pl.ds(at, 1), :] = real
                        out[pl.ds(at + plan.tiles, 1), :] = imag

        if targets == group:
            do_group(0)
        else:
            pl.loop(0, targets // group)(lambda g: do_group(g * group))

    return kernel, group, step


def downward_kernel(plan, n_wide):
    def kernel(received, cosines, sines, interp, rad, product, inner, twin):
        parent_dirs = cosines.shape[1]
        leaf_dirs = rad.shape[0]
        parents_dev = product.shape[0] // 8
        boxes = product.shape[0]
        parts = 2 * parents_dev
        lane = lax.broadcasted_iota(jnp.int32, (parts, plan.width), 1)
        inner[...] = jnp.zeros(inner.shape, F32)
        for w in range(n_wide):
            base = plan.dirs * w // 128 * 128
            shift = plan.dirs * w % 128
            span = -(-(shift + plan.dirs) // 128) * 128
            tiles = [
                received[pl.ds(w * parts * plan.tiles + k, parts, stride=plan.tiles), :]
                for k in range(plan.tiles)
            ]
            value = tiles[0] if plan.tiles == 1 else jnp.concatenate(tiles, 1)
            value = jnp.where(lane < plan.dirs, value, 0.0)
            if span > plan.width:
                value = jnp.concatenate([value, jnp.zeros((parts, span - plan.width), F32)], 1)
            if shift:
                value = pltpu.roll(value, shift, 1)
            span = min(value.shape[1], inner.shape[1] - base)
            inner[:, base : base + span] += value[:, 0:span]
        cs = cosines[...]
        sn = sines[...]
        reals, imags = [], []
        for p in range(parents_dev):
            in_real = inner[2 * p : 2 * p + 1, 0:parent_dirs]
            in_imag = inner[2 * p + 1 : 2 * p + 2, 0:parent_dirs]
            reals.append(cs * in_real + sn * in_imag)
            imags.append(cs * in_imag - sn * in_real)
        blank = jnp.zeros((128 - 2 * boxes, parent_dirs), F32)
        down = jnp.concatenate(
            reals + imags + [blank] + imags + [-r for r in reals] + [blank], 0
        ).astype(BF16)
        got = lax.dot_general(interp[...], down, NT, preferred_element_type=F32)
        twin[pl.ds(0, leaf_dirs, stride=2), :] = got[:, 0:128]
        twin[pl.ds(1, leaf_dirs, stride=2), :] = got[:, 128:256]
        flat = jnp.transpose(twin[...])[0 : 2 * boxes].astype(BF16)
        matrix = rad[...].reshape(2 * leaf_dirs, rad.shape[2])
        result = jnp.dot(flat, matrix, preferred_element_type=F32)
        product[:, 0, :] = result[0:boxes]
        product[:, 1, :] = result[boxes : 2 * boxes]

    return kernel


def on_device(
    coefficients, radiation, interpolation, angles, translations, sources, operators, counts
):
    boxes = coefficients.shape[0]
    parents_dev = boxes // 8
    leaf_dirs, parent_dirs = interpolation.shape
    bases = coefficients.shape[2]
    n_wide = lax.axis_size("wide")
    n_narrow = lax.axis_size("narrow")
    n_all = n_wide * n_narrow
    dirs = translations.shape[2]
    n_ops = translations.shape[0]
    plan = Plan(parents_dev * n_all, dirs, sources.shape[1], n_ops)
    rad = jnp.transpose(radiation, (2, 0, 1))
    table = jnp.transpose(translations, (1, 2, 0))
    chunk = 256
    vmem = pl.BlockSpec(memory_space=pltpu.VMEM)
    smem = pl.BlockSpec(memory_space=pltpu.SMEM)
    anywhere = pl.BlockSpec(memory_space=pl.ANY)

    send, cosines, sines = pl.pallas_call(
        upward_kernel(plan, n_wide, n_narrow, chunk),
        out_shape=(
            jax.ShapeDtypeStruct((n_all * parents_dev * plan.rows, 128), F32),
            jax.ShapeDtypeStruct(angles.shape, F32),
            jax.ShapeDtypeStruct(angles.shape, F32),
        ),
        in_specs=[smem, vmem, anywhere, anywhere, vmem, vmem, vmem],
        out_specs=(vmem, vmem, vmem),
        scratch_shapes=[
            pltpu.VMEM((leaf_dirs, 2, bases), BF16),
            pltpu.VMEM((leaf_dirs, parent_dirs), BF16),
            pltpu.VMEM((2 * leaf_dirs, 128), F32),
            pltpu.VMEM((2 * leaf_dirs, 128), F32),
            pltpu.VMEM((parents_dev, plan.code_width), F32),
            pltpu.VMEM((parents_dev, parent_dirs), F32),
            pltpu.VMEM((parents_dev, parent_dirs), F32),
            pltpu.SemaphoreType.DMA((parent_dirs // chunk + 1,)),
        ],
        compiler_params=pltpu.CompilerParams(vmem_limit_bytes=32 * MIB),
        name="upward",
    )(counts, coefficients, rad, interpolation, angles, sources, operators)

    send = send.reshape(n_all, parents_dev * plan.rows, 128)
    received = lax.all_to_all(send, ("wide", "narrow"), split_axis=0, concat_axis=0, tiled=True)
    received = received.reshape(-1, 128)

    body, group, step = translate_kernel(plan, n_wide, n_narrow, parents_dev)
    op_lanes = -(-n_ops // 128) * 128
    incoming = pl.pallas_call(
        body,
        out_shape=jax.ShapeDtypeStruct((n_wide * parents_dev * 2 * plan.tiles, 128), F32),
        in_specs=[vmem, vmem],
        out_specs=vmem,
        scratch_shapes=[
            pltpu.VMEM((2, plan.width, op_lanes), BF16),
            pltpu.VMEM((group * plan.parents, op_lanes), BF16),
            pltpu.VMEM((group * plan.parents, step), F32),
            pltpu.VMEM((group * plan.parents, step), F32),
        ],
        compiler_params=pltpu.CompilerParams(vmem_limit_bytes=24 * MIB),
        name="translate",
    )(table, received)

    incoming = incoming.reshape(n_wide, parents_dev * 2 * plan.tiles, 128)
    back = lax.all_to_all(incoming, "wide", split_axis=0, concat_axis=0, tiled=True)
    back = back.reshape(-1, 128)

    return pl.pallas_call(
        downward_kernel(plan, n_wide),
        out_shape=jax.ShapeDtypeStruct((boxes, 2, bases), F32),
        in_specs=[vmem] * 5,
        out_specs=vmem,
        scratch_shapes=[
            pltpu.VMEM((2 * parents_dev, parent_dirs + 128), F32),
            pltpu.VMEM((2 * leaf_dirs, 128), F32),
        ],
        compiler_params=pltpu.CompilerParams(vmem_limit_bytes=32 * MIB),
        name="downward",
    )(back, cosines, sines, interpolation, rad)


def solution(mesh):
    in_specs = (
        P(("wide", "narrow"), None, None),
        P(),
        P(),
        P(),
        P(None, None, "wide"),
        P(("wide", "narrow"), None),
        P(("wide", "narrow"), None),
        P(("wide", "narrow")),
    )
    out_specs = P(("wide", "narrow"), None, None)
    return jax.shard_map(
        on_device, mesh=mesh, in_specs=in_specs, out_specs=out_specs, check_vma=False
    )
```

time: 249 us -> 47.5 us (0.19)
  local copies, waits for them, and re-layouts: 140 us -> 7.84 us
  blocking collectives: 78.3 us -> 27.2 us
  other arithmetic: 13.1 us -> 0 us
  Pallas kernels: 0 us -> 12 us
  matrix products: 7.72 us -> 0 us
  starting transfers between devices: 7.25 us -> 0 us
    gather x12 -> x0, local copies, waits for them, and re-layouts: 108 us -> none  [the longest x3 26.9 us: translate(): oper_real = jnp.take(tab_real, operator_index, axis=0)]
    all_gather x3 -> x0, blocking collectives: 58.5 us -> none  [the longest x1 26.5 us: on_device(): lax.all_gather(operators, 'wide', axis=0, tiled=True)]
    all_to_all x1 -> x2, blocking collectives: 12 us -> 27.2 us  [the longest x1 17.7 us: on_device(): lax.all_to_all(send, ('wide', 'narrow'), split_axis=0, concat_axis=0, til...]
    pallas_call x0 -> x3, Pallas kernels: none -> 12 us  [the longest x1 6.48 us: on_device(): pl.pallas_call(upward_kernel(plan, n_wide, n_narrow, chunk), out_shape=(j...]
    reduce_sum x2 -> x0, other arithmetic: 11.2 us -> none  [the longest x1 11 us: translate(): jnp.sum(weight * (oper_real * pick_real - oper_imag * pick_imag), 1)]
    unnamed x1 -> x0, blocking collectives: 7.78 us -> none
    dot_general x10 -> x0, matrix products: 7.72 us -> none  [the longest x1 4.46 us: on_device(): lax.dot_general(downward.reshape(box_dev * 2, parent_dirs), interpolation...]
    slice x5 -> x0, local copies, waits for them, and re-layouts: 7.63 us -> none  [the longest x1 5.26 us: on_device(): rad_imag = radiation[1]]
  transfers between devices with their start and end apart: 1 -> 0, of which waited for: 0 -> 0; matrix products, arithmetic and copies ran while one was open for 24% -> 0% of each run, Pallas kernels for 0% -> 0%
where the time goes in v1:
time: 47.5 us; the launch traced here: 47.1 us
  blocking collectives  27.2 us (57%)
  Pallas kernels  12 us (25%)
  local copies, waits for them, and re-layouts  7.84 us (17%)
    all_to_all x1, blocking collectives, on_device(): lax.all_to_all(send, ('wide', 'narrow'), split_axis=0, concat_axis=0, til...  17.7 us
    all_to_all x1, blocking collectives, on_device(): lax.all_to_all(incoming, 'wide', split_axis=0, concat_axis=0, tiled=True)  9.51 us
    unnamed x18, local copies, waits for them, and re-layouts  7.84 us
    pallas_call x1, Pallas kernels, on_device(): pl.pallas_call(upward_kernel(plan, n_wide, n_narrow, chunk), out_shape=(j...  6.48 us
    pallas_call x1, Pallas kernels, on_device(): pl.pallas_call(downward_kernel(plan, n_wide), out_shape=jax.ShapeDtypeStr...  3.16 us
    pallas_call x1, Pallas kernels, on_device(): pl.pallas_call(body, out_shape=jax.ShapeDtypeStruct((n_wide * parents_dev...  2.37 us

profile of v1, /device:TPU:0, one launch (start us, length us, event | category | flops | bytes accessed | tf_op | source)
XLA Modules:
  0.0 47.1 jit_solution(5510932958069504309)
XLA Ops:
  0.0 0.0 copy-start
  0.0 2.7 %copy-done = bf16[882,3328]{1,0:T(8,128)(2,1)S(1)} copy-done((bf16[882,3328]{1,0:T(8,128)(2,1)S(1)}, bf16[882,3328]{1,0:T(8,128)(2,1)}, u32[]{:S(2)}) %copy-start) | copy-done | bytes 5870616
  2.7 0.0 copy-start.2
  2.7 1.5 %copy-done.2 = bf16[2,512,882]{1,0,2:T(2,128)(2,1)S(1)} copy-done((bf16[2,512,882]{1,0,2:T(2,128)(2,1)S(1)}, bf16[2,512,882]{1,0,2:T(2,128)(2,1)}, u32[]{:S(2)}) %copy-start.2) | copy-done | bytes 1806360
  4.2 0.0 copy-start.4
  4.2 0.9 %copy-done.4 = f32[8,3328]{1,0:T(8,128)S(1)} copy-done((f32[8,3328]{1,0:T(8,128)S(1)}, f32[8,3328]{1,0:T(8,128)}, u32[]{:S(2)}) %copy-start.4) | copy-done | bytes 106520
  5.1 0.0 copy-start.5
  5.1 0.8 %copy-done.5 = bf16[16,2,512]{2,1,0:T(2,128)(2,1)S(1)} copy-done((bf16[16,2,512]{2,1,0:T(2,128)(2,1)S(1)}, bf16[16,2,512]{2,1,0:T(2,128)(2,1)}, u32[]{:S(2)}) %copy-start.5) | copy-done | bytes 32792
  5.8 0.0 copy-start.6
  5.8 0.7 %copy-done.6 = s32[2,189]{1,0:T(2,128)S(1)} copy-done((s32[2,189]{1,0:T(2,128)S(1)}, s32[2,189]{1,0:T(2,128)}, u32[]{:S(2)}) %copy-start.6) | copy-done | bytes 1536
  6.5 0.0 copy-start.7
  6.5 0.7 %copy-done.7 = s32[2,189]{1,0:T(2,128)S(1)} copy-done((s32[2,189]{1,0:T(2,128)S(1)}, s32[2,189]{1,0:T(2,128)}, u32[]{:S(2)}) %copy-start.7) | copy-done | bytes 1536
  7.2 0.0 copy-start.8
  7.2 0.7 %copy-done.8 = s32[2]{0:T(128)S(1)} copy-done((s32[2]{0:T(128)S(1)}, s32[2]{0:T(128)}, u32[]{:S(2)}) %copy-start.8) | copy-done | bytes 32
  7.8 0.0 copy-start.3
  7.8 0.0 copy-start.1
  7.8 6.5 %upward.1 = (f32[512,128]{1,0:T(8,128)S(1)}, f32[8,3328]{1,0:T(8,128)S(1)}, f32[8,3328]{1,0:T(8,128)S(1)}) custom-call(s32[2]{0:T(128)S(1)} %copy-done.8, bf16[16,2,512]{2,1,0:T(2,128)(2,1)S(1)} %copy-done.5, bf16[882,2,512]{2,1,0:T(2,128)(2,1)S(1)} %bitcast.6, bf16[882,3328]{1,0:T(8,128)(2,1)S(1)} %copy-done, f32[8,3328]{1,0:T(8,128)S(1)} %copy-done.4, ...), custom_call_target="tpu_custom_call" | custom-call | tf_op jit(solution)/shard_map/upward/pallas_call | solution.py:291
  14.3 17.7 %all_to_all.10 = f32[32,16,128]{2,1,0:T(8,128)S(1)} all-to-all(f32[32,16,128]{2,1,0:T(8,128)S(1)} %bitcast.12), channel_id=1, replica_groups=mesh['wide'=8,'narrow'=4] {'wide','narrow'}, dimensions={0} | all-to-all | bytes 524288 | tf_op jit(solution)/shard_map/all_to_all | solution.py:315
  32.0 0.0 copy-done.3
  32.0 2.4 %translate.1 = f32[128,128]{1,0:T(8,128)S(1)} custom-call(f32[2,416,316]{2,1,0:T(8,128)S(1)} %bitcast.8, f32[512,128]{1,0:T(8,128)S(1)} %bitcast.9), custom_call_target="tpu_custom_call" | custom-call | tf_op jit(solution)/shard_map/translate/pallas_call | solution.py:320
  34.4 9.5 %all_to_all.11 = f32[8,16,128]{2,1,0:T(8,128)S(1)} all-to-all(f32[8,16,128]{2,1,0:T(8,128)S(1)} %bitcast.11), channel_id=1, replica_groups=mesh['wide'=8,'narrow'=4] {'wide'}, dimensions={0} | all-to-all | bytes 131072 | tf_op jit(solution)/shard_map/all_to_all | solution.py:336
  43.9 0.0 copy-done.1
  43.9 3.2 %downward.1 = f32[16,2,512]{2,1,0:T(2,128)} custom-call(f32[128,128]{1,0:T(8,128)S(1)} %bitcast.10, f32[8,3328]{1,0:T(8,128)S(1)} %get-tuple-element.9.cosines, f32[8,3328]{1,0:T(8,128)S(1)} %get-tuple-element.10.sines, bf16[882,3328]{1,0:T(8,128)(2,1)S(1)} %copy-done.1, bf16[882,2,512]{2,1,0:T(2,128)(2,1)S(1)} %bitcast.7), custom_call_target="tpu_custom_call" | custom-call | tf_op jit(solution)/shard_map/downward/pallas_call | solution.py:339
Async XLA Ops:
  0.0 2.7 %copy-start = (bf16[882,3328]{1,0:T(8,128)(2,1)S(1)}, bf16[882,3328]{1,0:T(8,128)(2,1)}, u32[]{:S(2)}) copy-start(bf16[882,3328]{1,0:T(8,128)(2,1)} %interp.1) | copy-start | bytes 17611780
  2.7 1.5 %copy-start.2 = (bf16[2,512,882]{1,0,2:T(2,128)(2,1)S(1)}, bf16[2,512,882]{1,0,2:T(2,128)(2,1)}, u32[]{:S(2)}) copy-start(bf16[2,512,882]{1,0,2:T(2,128)(2,1)} %param.9) | copy-start | bytes 5419012
  4.2 0.9 %copy-start.4 = (f32[8,3328]{1,0:T(8,128)S(1)}, f32[8,3328]{1,0:T(8,128)}, u32[]{:S(2)}) copy-start(f32[8,3328]{1,0:T(8,128)} %angles.1) | copy-start | bytes 319492
  5.1 0.8 %copy-start.5 = (bf16[16,2,512]{2,1,0:T(2,128)(2,1)S(1)}, bf16[16,2,512]{2,1,0:T(2,128)(2,1)}, u32[]{:S(2)}) copy-start(bf16[16,2,512]{2,1,0:T(2,128)(2,1)} %coef.1) | copy-start | bytes 98308
  5.8 0.7 %copy-start.6 = (s32[2,189]{1,0:T(2,128)S(1)}, s32[2,189]{1,0:T(2,128)}, u32[]{:S(2)}) copy-start(s32[2,189]{1,0:T(2,128)} %sources.1) | copy-start | bytes 4540
  6.5 0.7 %copy-start.7 = (s32[2,189]{1,0:T(2,128)S(1)}, s32[2,189]{1,0:T(2,128)}, u32[]{:S(2)}) copy-start(s32[2,189]{1,0:T(2,128)} %operators.1) | copy-start | bytes 4540
  7.2 0.7 %copy-start.8 = (s32[2]{0:T(128)S(1)}, s32[2]{0:T(128)}, u32[]{:S(2)}) copy-start(s32[2]{0:T(128)} %counts.1) | copy-start | bytes 28
  7.8 24.2 %copy-start.3 = (f32[316,2,416]{0,2,1:T(8,128)S(1)}, f32[316,2,416]{0,2,1:T(8,128)}, u32[]{:S(2)}) copy-start(f32[316,2,416]{0,2,1:T(8,128)} %param.12) | copy-start | bytes 3154948
  7.8 36.1 %copy-start.1 = (bf16[882,3328]{1,0:T(8,128)(2,1)S(1)}, bf16[882,3328]{1,0:T(8,128)(2,1)}, u32[]{:S(2)}) copy-start(bf16[882,3328]{1,0:T(8,128)(2,1)} %interp.1) | copy-start | bytes 17611780

commit v2 on v1

--- a/solution.py
+++ b/solution.py
@@ -71,29 +71,42 @@
     return (first + second).astype(BF16)
 
 
-def upward_kernel(plan, n_wide, n_narrow, chunk):
+def upward_kernel(plan, n_wide, n_narrow, cuts):
     def kernel(
-        counts, coef, rad_hbm, interp_hbm, angles, sources, operators,
+        counts_hbm, coef_hbm, rad_hbm, interp_hbm, angles_hbm, sources_hbm, operators_hbm,
         send, cos_out, sin_out,
-        rad, interp, even, odd, codes, real_buf, imag_buf, sems,
+        counts, coef, rad, interp, angles, sources, operators,
+        even, odd, codes, real_buf, imag_buf, sems,
     ):
         parent_dirs = angles.shape[1]
         leaf_dirs = rad.shape[0]
         boxes = coef.shape[0]
         parents_dev = boxes // 8
-        n_chunks = parent_dirs // chunk
-        rad_copy = pltpu.make_async_copy(rad_hbm, rad, sems.at[n_chunks])
-        rad_copy.start()
+        n_chunks = len(cuts) - 1
+        first = []
+        for source, target in (
+            (angles_hbm, angles),
+            (coef_hbm, coef),
+            (rad_hbm, rad),
+            (sources_hbm, sources),
+            (operators_hbm, operators),
+            (counts_hbm, counts),
+        ):
+            first.append(pltpu.make_async_copy(source, target, sems.at[n_chunks + len(first)]))
+            first[-1].start()
         copies = []
         for c in range(n_chunks):
-            cut = (slice(None), pl.ds(c * chunk, chunk))
+            cut = (slice(None), pl.ds(cuts[c], cuts[c + 1] - cuts[c]))
             copies.append(pltpu.make_async_copy(interp_hbm.at[cut], interp.at[cut], sems.at[c]))
             copies[-1].start()
 
+        first[0].wait()
         sines, cosines = sin_cos(angles[...])
         sin_out[...] = sines
         cos_out[...] = cosines
 
+        for copy in first[3:]:
+            copy.wait()
         code = sources[...] * (1 << plan.bits) + operators[...]
         at = lax.broadcasted_iota(jnp.int32, code.shape, 1)
         parent = lax.broadcasted_iota(jnp.int32, code.shape, 0)
@@ -103,12 +116,13 @@
         codes[...] = jnp.full(codes.shape, -1.0, F32)
         codes[:, 0 : plan.length] = jnp.where(at < limit, code, -1).astype(F32)
 
+        first[1].wait()
         rows = coef[...].reshape(2 * boxes, coef.shape[2])
         plain = jnp.dot(arrange(boxes, False), rows, preferred_element_type=F32).astype(BF16)
         turned = jnp.dot(arrange(boxes, True), rows, preferred_element_type=F32).astype(BF16)
         weights = jnp.concatenate([plain, turned], 0)
 
-        rad_copy.wait()
+        first[2].wait()
         matrix = rad[...].reshape(2 * leaf_dirs, rad.shape[2])
         both = lax.dot_general(matrix, weights, NT, preferred_element_type=F32)
         even[...] = both[:, 0:128]
@@ -116,25 +130,19 @@
         leaf_t = even[pl.ds(0, leaf_dirs, stride=2), :] + odd[pl.ds(1, leaf_dirs, stride=2), :]
         leaf = jnp.transpose(leaf_t)[0 : 2 * boxes].astype(BF16)
 
-        for c in range(n_chunks):
-            copies[c].wait()
-            cut = slice(c * chunk, (c + 1) * chunk)
-            up = jnp.dot(leaf, interp[:, cut], preferred_element_type=F32)
-            cs = cos_out[:, cut]
-            sn = sin_out[:, cut]
-            for p in range(parents_dev):
-                up_real = up[8 * p : 8 * p + 8]
-                up_imag = up[boxes + 8 * p : boxes + 8 * p + 8]
-                real_buf[p : p + 1, cut] = jnp.sum(cs * up_real - sn * up_imag, 0, keepdims=True)
-                imag_buf[p : p + 1, cut] = jnp.sum(cs * up_imag + sn * up_real, 0, keepdims=True)
-
         lane = lax.broadcasted_iota(jnp.int32, (parents_dev, 128), 1)
         tails = {}
-        for tile, start, count, first in plan.pieces:
-            turn = (start - first) % plan.code_width
+        for tile, start, count, first_entry in plan.pieces:
+            turn = (start - first_entry) % plan.code_width
             moved = codes[...] if turn == 0 else pltpu.roll(codes[...], turn, 1)
             tails[tile] = (moved[:, 0:128], (lane >= start) & (lane < start + count))
-        for w in range(n_wide):
+
+        def put(w, tile, piece):
+            for n in range(n_narrow):
+                first_row = (w * n_narrow + n) * parents_dev * plan.rows + tile
+                send[pl.ds(first_row, parents_dev, stride=plan.rows), :] = piece
+
+        def pack(w):
             base = plan.dirs * w // 128 * 128
             shift = plan.dirs * w % 128
             span = -(-(shift + plan.dirs) // 128) * 128
@@ -150,15 +158,26 @@
                         piece = jnp.where(lane < plan.dirs - 128 * k, piece, -1.0)
                     if tile in tails:
                         piece = jnp.where(tails[tile][1], tails[tile][0], piece)
-                    for n in range(n_narrow):
-                        first = (w * n_narrow + n) * parents_dev * plan.rows + tile
-                        send[pl.ds(first, parents_dev, stride=plan.rows), :] = piece
+                    put(w, tile, piece)
             for e in range(plan.extra):
                 tile = 2 * plan.tiles + e
-                piece = jnp.where(tails[tile][1], tails[tile][0], -1.0)
-                for n in range(n_narrow):
-                    first = (w * n_narrow + n) * parents_dev * plan.rows + tile
-                    send[pl.ds(first, parents_dev, stride=plan.rows), :] = piece
+                put(w, tile, jnp.where(tails[tile][1], tails[tile][0], -1.0))
+
+        packed = 0
+        for c in range(n_chunks):
+            copies[c].wait()
+            cut = slice(cuts[c], cuts[c + 1])
+            up = jnp.dot(leaf, interp[:, cut], preferred_element_type=F32)
+            cs = cos_out[:, cut]
+            sn = sin_out[:, cut]
+            for p in range(parents_dev):
+                up_real = up[8 * p : 8 * p + 8]
+                up_imag = up[boxes + 8 * p : boxes + 8 * p + 8]
+                real_buf[p : p + 1, cut] = jnp.sum(cs * up_real - sn * up_imag, 0, keepdims=True)
+                imag_buf[p : p + 1, cut] = jnp.sum(cs * up_imag + sn * up_real, 0, keepdims=True)
+            while packed < n_wide and -(-plan.dirs * (packed + 1) // 128) * 128 <= cuts[c + 1]:
+                pack(packed)
+                packed += 1
 
     return kernel
 
@@ -283,31 +302,36 @@
     plan = Plan(parents_dev * n_all, dirs, sources.shape[1], n_ops)
     rad = jnp.transpose(radiation, (2, 0, 1))
     table = jnp.transpose(translations, (1, 2, 0))
-    chunk = 256
+    cuts = [0, 1664]
+    cuts = [c for c in cuts if c < parent_dirs] + [parent_dirs]
     vmem = pl.BlockSpec(memory_space=pltpu.VMEM)
-    smem = pl.BlockSpec(memory_space=pltpu.SMEM)
     anywhere = pl.BlockSpec(memory_space=pl.ANY)
 
     send, cosines, sines = pl.pallas_call(
-        upward_kernel(plan, n_wide, n_narrow, chunk),
+        upward_kernel(plan, n_wide, n_narrow, cuts),
         out_shape=(
             jax.ShapeDtypeStruct((n_all * parents_dev * plan.rows, 128), F32),
             jax.ShapeDtypeStruct(angles.shape, F32),
             jax.ShapeDtypeStruct(angles.shape, F32),
         ),
-        in_specs=[smem, vmem, anywhere, anywhere, vmem, vmem, vmem],
+        in_specs=[anywhere] * 7,
         out_specs=(vmem, vmem, vmem),
         scratch_shapes=[
+            pltpu.SMEM((parents_dev,), jnp.int32),
+            pltpu.VMEM((boxes, 2, bases), BF16),
             pltpu.VMEM((leaf_dirs, 2, bases), BF16),
             pltpu.VMEM((leaf_dirs, parent_dirs), BF16),
+            pltpu.VMEM(angles.shape, F32),
+            pltpu.VMEM(sources.shape, jnp.int32),
+            pltpu.VMEM(operators.shape, jnp.int32),
             pltpu.VMEM((2 * leaf_dirs, 128), F32),
             pltpu.VMEM((2 * leaf_dirs, 128), F32),
             pltpu.VMEM((parents_dev, plan.code_width), F32),
             pltpu.VMEM((parents_dev, parent_dirs), F32),
             pltpu.VMEM((parents_dev, parent_dirs), F32),
-            pltpu.SemaphoreType.DMA((parent_dirs // chunk + 1,)),
+            pltpu.SemaphoreType.DMA((len(cuts) + 5,)),
         ],
-        compiler_params=pltpu.CompilerParams(vmem_limit_bytes=32 * MIB),
+        compiler_params=pltpu.CompilerParams(vmem_limit_bytes=56 * MIB),
         name="upward",
     )(counts, coefficients, rad, interpolation, angles, sources, operators)
 

time: 47.5 us -> 38.8 us (0.82)
  local copies, waits for them, and re-layouts: 7.84 us -> 0.02 us
  Pallas kernels: 12 us -> 11 us
    unnamed x18 -> x10, local copies, waits for them, and re-layouts: 7.84 us -> 0.02 us
    pallas_call x1, Pallas kernels: 6.48 us -> 5.49 us  [on_device(): pl.pallas_call(upward_kernel(plan, n_wide, n_narrow, cuts), out_shape=(ja...]
where the time goes in v2:
time: 38.8 us; the launch traced here: 38.5 us
  blocking collectives  27.4 us (71%)
  Pallas kernels  11 us (28%)
    all_to_all x1, blocking collectives, on_device(): lax.all_to_all(send, ('wide', 'narrow'), split_axis=0, concat_axis=0, til...  17.9 us
    all_to_all x1, blocking collectives, on_device(): lax.all_to_all(incoming, 'wide', split_axis=0, concat_axis=0, tiled=True)  9.51 us
    pallas_call x1, Pallas kernels, on_device(): pl.pallas_call(upward_kernel(plan, n_wide, n_narrow, cuts), out_shape=(ja...  5.49 us
    pallas_call x1, Pallas kernels, on_device(): pl.pallas_call(downward_kernel(plan, n_wide), out_shape=jax.ShapeDtypeStr...  3.13 us
    pallas_call x1, Pallas kernels, on_device(): pl.pallas_call(body, out_shape=jax.ShapeDtypeStruct((n_wide * parents_dev...  2.37 us

profile of v2, /device:TPU:0, one launch (start us, length us, event | category | flops | bytes accessed | tf_op | source)
XLA Modules:
  0.0 38.5 jit_solution(2413418036341222909)
XLA Ops:
  0.0 0.0 copy-start.2
  0.0 0.0 copy-start
  0.0 5.5 %upward.1 = (f32[512,128]{1,0:T(8,128)}, f32[8,3328]{1,0:T(8,128)}, f32[8,3328]{1,0:T(8,128)}) custom-call(s32[2]{0:T(128)} %counts_hbm.1, bf16[16,2,512]{2,1,0:T(2,128)(2,1)} %coef_hbm.1, bf16[882,2,512]{2,1,0:T(2,128)(2,1)} %bitcast.6, bf16[882,3328]{1,0:T(8,128)(2,1)} %interp.1, f32[8,3328]{1,0:T(8,128)} %angles_hbm.1, s32[2,189]{1,0:T(2,128)} %sources_hbm.1, ...), custom_call_target="tpu_custom_call" | custom-call | tf_op jit(solution)/shard_map/upward/pallas_call | solution.py:310
  5.5 0.0 copy-start.1
  5.5 0.0 copy-start.3
  5.5 0.0 copy-start.4
  5.5 17.9 %all_to_all.10 = f32[32,16,128]{2,1,0:T(8,128)S(1)} all-to-all(f32[32,16,128]{2,1,0:T(8,128)} %bitcast.12), channel_id=1, replica_groups=mesh['wide'=8,'narrow'=4] {'wide','narrow'}, dimensions={0} | all-to-all | bytes 524288 | tf_op jit(solution)/shard_map/all_to_all | solution.py:339
  23.5 0.0 copy-done.2
  23.5 2.4 %translate.1 = f32[128,128]{1,0:T(8,128)S(1)} custom-call(f32[2,416,316]{2,1,0:T(8,128)S(1)} %bitcast.8, f32[512,128]{1,0:T(8,128)S(1)} %bitcast.9), custom_call_target="tpu_custom_call" | custom-call | tf_op jit(solution)/shard_map/translate/pallas_call | solution.py:344
  25.8 9.5 %all_to_all.11 = f32[8,16,128]{2,1,0:T(8,128)S(1)} all-to-all(f32[8,16,128]{2,1,0:T(8,128)S(1)} %bitcast.11), channel_id=1, replica_groups=mesh['wide'=8,'narrow'=4] {'wide'}, dimensions={0} | all-to-all | bytes 131072 | tf_op jit(solution)/shard_map/all_to_all | solution.py:360
  35.3 0.0 copy-done
  35.3 0.0 copy-done.1
  35.3 0.0 copy-done.3
  35.4 0.0 copy-done.4
  35.4 3.1 %downward.1 = f32[16,2,512]{2,1,0:T(2,128)} custom-call(f32[128,128]{1,0:T(8,128)S(1)} %bitcast.10, f32[8,3328]{1,0:T(8,128)S(1)} %copy-done.3, f32[8,3328]{1,0:T(8,128)S(1)} %copy-done.4, bf16[882,3328]{1,0:T(8,128)(2,1)S(1)} %copy-done, bf16[882,2,512]{2,1,0:T(2,128)(2,1)S(1)} %bitcast.7), custom_call_target="tpu_custom_call" | custom-call | tf_op jit(solution)/shard_map/downward/pallas_call | solution.py:363
Async XLA Ops:
  0.0 23.5 %copy-start.2 = (f32[316,2,416]{0,2,1:T(8,128)S(1)}, f32[316,2,416]{0,2,1:T(8,128)}, u32[]{:S(2)}) copy-start(f32[316,2,416]{0,2,1:T(8,128)} %param.12) | copy-start | bytes 3154948
  0.0 35.3 %copy-start = (bf16[882,3328]{1,0:T(8,128)(2,1)S(1)}, bf16[882,3328]{1,0:T(8,128)(2,1)}, u32[]{:S(2)}) copy-start(bf16[882,3328]{1,0:T(8,128)(2,1)} %interp.1) | copy-start | bytes 17611780
  5.5 29.8 %copy-start.1 = (bf16[2,512,882]{1,0,2:T(2,128)(2,1)S(1)}, bf16[2,512,882]{1,0,2:T(2,128)(2,1)}, u32[]{:S(2)}) copy-start(bf16[2,512,882]{1,0,2:T(2,128)(2,1)} %param.9) | copy-start | bytes 5419012
  5.5 29.8 %copy-start.3 = (f32[8,3328]{1,0:T(8,128)S(1)}, f32[8,3328]{1,0:T(8,128)}, u32[]{:S(2)}) copy-start(f32[8,3328]{1,0:T(8,128)} %get-tuple-element.9.cosines) | copy-start | bytes 319492
  5.5 29.8 %copy-start.4 = (f32[8,3328]{1,0:T(8,128)S(1)}, f32[8,3328]{1,0:T(8,128)}, u32[]{:S(2)}) copy-start(f32[8,3328]{1,0:T(8,128)} %get-tuple-element.10.sines) | copy-start | bytes 319492

commit v3 on v2

--- a/solution.py
+++ b/solution.py
@@ -83,6 +83,7 @@
         boxes = coef.shape[0]
         parents_dev = boxes // 8
         n_chunks = len(cuts) - 1
+        half = -(-leaf_dirs // 16) * 16
         first = []
         for source, target in (
             (angles_hbm, angles),
@@ -124,9 +125,12 @@
 
         first[2].wait()
         matrix = rad[...].reshape(2 * leaf_dirs, rad.shape[2])
-        both = lax.dot_general(matrix, weights, NT, preferred_element_type=F32)
-        even[...] = both[:, 0:128]
-        odd[...] = both[:, 128:256]
+        weights_t = jnp.transpose(weights)
+        for a in range(0, 2 * leaf_dirs, half):
+            z = min(a + half, 2 * leaf_dirs)
+            both = jnp.dot(matrix[a:z], weights_t, preferred_element_type=F32)
+            even[a:z, :] = both[:, 0:128]
+            odd[a:z, :] = both[:, 128:256]
         leaf_t = even[pl.ds(0, leaf_dirs, stride=2), :] + odd[pl.ds(1, leaf_dirs, stride=2), :]
         leaf = jnp.transpose(leaf_t)[0 : 2 * boxes].astype(BF16)
 
@@ -192,8 +196,10 @@
         table[...] = jnp.zeros(table.shape, BF16)
         table[:, 0 : plan.dirs, 0 : plan.ops] = table_in[...].astype(BF16)
         lane = lax.broadcasted_iota(jnp.int32, (1, 128), 1)
-        source_at = lax.broadcasted_iota(jnp.int32, (plan.parents, 128), 0)
-        op_at = lax.broadcasted_iota(jnp.int32, (table.shape[2], 128), 0)
+        highs = table.shape[2] // 128
+        kind = BF16 if highs * plan.parents <= 256 else F32
+        key_at = lax.broadcasted_iota(jnp.int32, (highs * plan.parents, 128), 0).astype(kind)
+        low_at = lax.broadcasted_iota(jnp.int32, (128, 128), 0).astype(BF16)
 
         def do_group(first_target):
             for i in range(group):
@@ -201,20 +207,26 @@
                 w = target // parents_dev
                 p = target % parents_dev
                 row = ((w * n_narrow + mine) * parents_dev + p) * plan.rows
-                hits, picks = [], []
+                keys, lows = [], []
                 for tile, start, count, _ in plan.pieces:
                     code = received[pl.ds(row + tile, 1), :]
                     code = jnp.where((lane >= start) & (lane < start + count), code, -1.0).astype(jnp.int32)
-                    hits.append(jnp.where(source_at == (code >> plan.bits), 1.0, 0.0).astype(BF16))
-                    picks.append(jnp.where(op_at == (code & ((1 << plan.bits) - 1)), 1.0, 0.0).astype(BF16))
+                    op = code & ((1 << plan.bits) - 1)
+                    key = jnp.where(code < 0, -1, (op >> 7) * plan.parents + (code >> plan.bits))
+                    keys.append(jnp.where(key_at == key.astype(kind), jnp.ones((), kind), jnp.zeros((), kind)).astype(BF16))
+                    lows.append(jnp.where(low_at == (op & 127).astype(BF16), jnp.ones((), BF16), jnp.zeros((), BF16)))
                 count_of = lax.dot_general(
-                    jnp.concatenate(hits, 1), jnp.concatenate(picks, 1), NT, preferred_element_type=F32
-                )
-                tally[i * plan.parents : (i + 1) * plan.parents, :] = count_of.astype(BF16)
+                    jnp.concatenate(keys, 1), jnp.concatenate(lows, 1), NT, preferred_element_type=F32
+                ).astype(BF16)
+                own = slice(i * plan.parents, (i + 1) * plan.parents)
+                for h in range(highs):
+                    tally[own, 128 * h : 128 * h + 128] = count_of[h * plan.parents : (h + 1) * plan.parents]
             for j in range(plan.width // step):
                 cut = slice(j * step, (j + 1) * step)
-                a_real[...] = lax.dot_general(tally[...], table[0, cut, :], NT, preferred_element_type=F32)
-                a_imag[...] = lax.dot_general(tally[...], table[1, cut, :], NT, preferred_element_type=F32)
+                for a in range(0, tally.shape[0], 512):
+                    z = min(a + 512, tally.shape[0])
+                    a_real[a:z, :] = lax.dot_general(tally[a:z, :], table[0, cut, :], NT, preferred_element_type=F32)
+                    a_imag[a:z, :] = lax.dot_general(tally[a:z, :], table[1, cut, :], NT, preferred_element_type=F32)
                 for q in range(step // 128):
                     k = j * (step // 128) + q
                     lanes = slice(128 * q, 128 * q + 128)
@@ -275,7 +287,15 @@
         down = jnp.concatenate(
             reals + imags + [blank] + imags + [-r for r in reals] + [blank], 0
         ).astype(BF16)
-        got = lax.dot_general(interp[...], down, NT, preferred_element_type=F32)
+        down_t = jnp.transpose(down)
+        quarter = -(-leaf_dirs // 64) * 16
+        got = jnp.concatenate(
+            [
+                jnp.dot(interp[a : min(a + quarter, leaf_dirs), :], down_t, preferred_element_type=F32)
+                for a in range(0, leaf_dirs, quarter)
+            ],
+            0,
+        )
         twin[pl.ds(0, leaf_dirs, stride=2), :] = got[:, 0:128]
         twin[pl.ds(1, leaf_dirs, stride=2), :] = got[:, 128:256]
         flat = jnp.transpose(twin[...])[0 : 2 * boxes].astype(BF16)

time: 38.8 us -> 37.3 us (0.961)
  Pallas kernels: 11 us -> 9.59 us
    pallas_call x1, Pallas kernels: 2.37 us -> 1.81 us  [on_device(): pl.pallas_call(body, out_shape=jax.ShapeDtypeStruct((n_wide * parents_dev...]
    pallas_call x1, Pallas kernels: 5.49 us -> 5.02 us  [on_device(): pl.pallas_call(upward_kernel(plan, n_wide, n_narrow, cuts), out_shape=(ja...]
where the time goes in v3:
time: 37.3 us; the launch traced here: 37.1 us
  blocking collectives  27.4 us (73%)
  Pallas kernels  9.59 us (26%)
    all_to_all x1, blocking collectives, on_device(): lax.all_to_all(send, ('wide', 'narrow'), split_axis=0, concat_axis=0, til...  17.9 us
    all_to_all x1, blocking collectives, on_device(): lax.all_to_all(incoming, 'wide', split_axis=0, concat_axis=0, tiled=True)  9.51 us
    pallas_call x1, Pallas kernels, on_device(): pl.pallas_call(upward_kernel(plan, n_wide, n_narrow, cuts), out_shape=(ja...  5.02 us
    pallas_call x1, Pallas kernels, on_device(): pl.pallas_call(downward_kernel(plan, n_wide), out_shape=jax.ShapeDtypeStr...  2.75 us
    pallas_call x1, Pallas kernels, on_device(): pl.pallas_call(body, out_shape=jax.ShapeDtypeStruct((n_wide * parents_dev...  1.81 us

profile of v3, /device:TPU:0, one launch (start us, length us, event | category | flops | bytes accessed | tf_op | source)
XLA Modules:
  0.0 37.1 jit_solution(6559631985285738120)
XLA Ops:
  0.0 0.0 copy-start.2
  0.0 0.0 copy-start
  0.0 5.0 %upward.1 = (f32[512,128]{1,0:T(8,128)}, f32[8,3328]{1,0:T(8,128)}, f32[8,3328]{1,0:T(8,128)}) custom-call(s32[2]{0:T(128)} %counts_hbm.1, bf16[16,2,512]{2,1,0:T(2,128)(2,1)} %coef_hbm.1, bf16[882,2,512]{2,1,0:T(2,128)(2,1)} %bitcast.6, bf16[882,3328]{1,0:T(8,128)(2,1)} %interp.1, f32[8,3328]{1,0:T(8,128)} %angles_hbm.1, s32[2,189]{1,0:T(2,128)} %sources_hbm.1, ...), custom_call_target="tpu_custom_call" | custom-call | tf_op jit(solution)/shard_map/upward/pallas_call | solution.py:330
  5.0 0.0 copy-start.1
  5.0 0.0 copy-start.3
  5.1 0.0 copy-start.4
  5.1 17.9 %all_to_all.10 = f32[32,16,128]{2,1,0:T(8,128)S(1)} all-to-all(f32[32,16,128]{2,1,0:T(8,128)} %bitcast.12), channel_id=1, replica_groups=mesh['wide'=8,'narrow'=4] {'wide','narrow'}, dimensions={0} | all-to-all | bytes 524288 | tf_op jit(solution)/shard_map/all_to_all | solution.py:359
  23.0 0.0 copy-done.2
  23.0 1.8 %translate.1 = f32[128,128]{1,0:T(8,128)S(1)} custom-call(f32[2,416,316]{2,1,0:T(8,128)S(1)} %bitcast.8, f32[512,128]{1,0:T(8,128)S(1)} %bitcast.9), custom_call_target="tpu_custom_call" | custom-call | tf_op jit(solution)/shard_map/translate/pallas_call | solution.py:364
  24.8 9.5 %all_to_all.11 = f32[8,16,128]{2,1,0:T(8,128)S(1)} all-to-all(f32[8,16,128]{2,1,0:T(8,128)S(1)} %bitcast.11), channel_id=1, replica_groups=mesh['wide'=8,'narrow'=4] {'wide'}, dimensions={0} | all-to-all | bytes 131072 | tf_op jit(solution)/shard_map/all_to_all | solution.py:380
  34.3 0.0 copy-done
  34.3 0.0 copy-done.1
  34.3 0.0 copy-done.3
  34.3 0.0 copy-done.4
  34.3 2.7 %downward.1 = f32[16,2,512]{2,1,0:T(2,128)} custom-call(f32[128,128]{1,0:T(8,128)S(1)} %bitcast.10, f32[8,3328]{1,0:T(8,128)S(1)} %copy-done.3, f32[8,3328]{1,0:T(8,128)S(1)} %copy-done.4, bf16[882,3328]{1,0:T(8,128)(2,1)S(1)} %copy-done, bf16[882,2,512]{2,1,0:T(2,128)(2,1)S(1)} %bitcast.7), custom_call_target="tpu_custom_call" | custom-call | tf_op jit(solution)/shard_map/downward/pallas_call | solution.py:383
Async XLA Ops:
  0.0 23.0 %copy-start.2 = (f32[316,2,416]{0,2,1:T(8,128)S(1)}, f32[316,2,416]{0,2,1:T(8,128)}, u32[]{:S(2)}) copy-start(f32[316,2,416]{0,2,1:T(8,128)} %param.12) | copy-start | bytes 3154948
  0.0 34.3 %copy-start = (bf16[882,3328]{1,0:T(8,128)(2,1)S(1)}, bf16[882,3328]{1,0:T(8,128)(2,1)}, u32[]{:S(2)}) copy-start(bf16[882,3328]{1,0:T(8,128)(2,1)} %interp.1) | copy-start | bytes 17611780
  5.0 29.3 %copy-start.1 = (bf16[2,512,882]{1,0,2:T(2,128)(2,1)S(1)}, bf16[2,512,882]{1,0,2:T(2,128)(2,1)}, u32[]{:S(2)}) copy-start(bf16[2,512,882]{1,0,2:T(2,128)(2,1)} %param.9) | copy-start | bytes 5419012
  5.0 29.3 %copy-start.3 = (f32[8,3328]{1,0:T(8,128)S(1)}, f32[8,3328]{1,0:T(8,128)}, u32[]{:S(2)}) copy-start(f32[8,3328]{1,0:T(8,128)} %get-tuple-element.9.cosines) | copy-start | bytes 319492
  5.1 29.3 %copy-start.4 = (f32[8,3328]{1,0:T(8,128)S(1)}, f32[8,3328]{1,0:T(8,128)}, u32[]{:S(2)}) copy-start(f32[8,3328]{1,0:T(8,128)} %get-tuple-element.10.sines) | copy-start | bytes 319492

commit v4 on v3

--- a/solution.py
+++ b/solution.py
@@ -12,30 +12,72 @@
 
 
 class Plan:
-    def __init__(self, parents, dirs, length, ops):
-        self.parents = parents
+    def __init__(self, own, n_wide, n_narrow, dirs, length, ops):
+        self.own = own
+        self.n_wide = n_wide
+        self.n_narrow = n_narrow
+        self.devices = n_wide * n_narrow
+        self.parents = own * self.devices
+        first = n_wide * 5 // 8
+        self.order = list(range(first, -1, -1)) + list(range(first + 1, n_wide))
+        self.cores = 2 if n_narrow % 2 == 0 else 1
+        self.pairs = n_narrow // self.cores
+        self.peers = n_wide * self.pairs
         self.dirs = dirs
         self.length = length
         self.ops = ops
+        self.full = dirs // 128
+        self.rest = dirs % 128
         self.tiles = -(-dirs // 128)
         self.width = 128 * self.tiles
-        spare = self.width - dirs
-        used = dirs - 128 * (self.tiles - 1)
-        self.bits = (ops - 1).bit_length()
-        if 2 * spare >= length:
-            self.extra = 0
-            self.pieces = [
-                (self.tiles - 1, used, spare, 0),
-                (2 * self.tiles - 1, used, length - spare, spare),
-            ]
-        else:
-            self.extra = -(-length // 128)
-            self.pieces = [
-                (2 * self.tiles + e, 0, min(128, length - 128 * e), 128 * e)
-                for e in range(self.extra)
-            ]
-        self.rows = 2 * self.tiles + self.extra
-        self.code_width = -(-length // 128) * 128
+        self.bits = ops.bit_length()
+        entry_bits = self.bits + (self.parents - 1).bit_length()
+        self.none = (1 << entry_bits) - 1
+        self.rest_row = own * 2 * self.full
+        self.shared = 2 * own * self.rest <= 128
+        rest_rows = 0 if not self.rest else 1 if self.shared else 2 * own
+        self.list_row = self.rest_row + rest_rows
+        self.dense = entry_bits <= 15 and length <= 192
+        self.entry_tiles = 2 if self.dense else -(-length // 128)
+        self.list_rows = 1 if self.dense else self.entry_tiles
+        self.rows = self.list_row + own * self.list_rows
+
+    def rest_at(self, p, part):
+        if self.shared:
+            return self.rest_row, (2 * p + part) * self.rest
+        return self.rest_row + 2 * p + part, 0
+
+    def groups(self):
+        return [
+            [w * self.n_narrow + pair * self.cores + core for w in self.order for pair in range(self.pairs)]
+            for core in range(self.cores)
+        ]
+
+    def place(self, source):
+        narrow_shift = self.own.bit_length() - 1
+        device = source >> narrow_shift
+        place = jnp.zeros(source.shape, jnp.int32)
+        for i, w in enumerate(self.order):
+            for pair in range(self.pairs):
+                for core in range(self.cores):
+                    flat = w * self.n_narrow + pair * self.cores + core
+                    block = core * self.peers + i * self.pairs + pair
+                    place = jnp.where(device == flat, block, place)
+        return (source & (self.own - 1)) * self.devices + place
+
+    def encode(self, entries, lane):
+        if not self.dense:
+            return entries
+        first, third = entries
+        low = jnp.where(lane < 64, third & 255, pltpu.roll(third, 64, 1) >> 8)
+        return [first * 256 + low]
+
+    def decode(self, words, lane):
+        if not self.dense:
+            return words
+        low = words[0] & 255
+        third = low + (pltpu.roll(low, 64, 1) << 8)
+        return [words[0] >> 8, jnp.where(lane < 64, third, self.none)]
 
 
 def sin_cos(angle):
@@ -71,7 +113,7 @@
     return (first + second).astype(BF16)
 
 
-def upward_kernel(plan, n_wide, n_narrow, cuts):
+def upward_kernel(plan, cuts):
     def kernel(
         counts_hbm, coef_hbm, rad_hbm, interp_hbm, angles_hbm, sources_hbm, operators_hbm,
         send, cos_out, sin_out,
@@ -108,14 +150,14 @@
 
         for copy in first[3:]:
             copy.wait()
-        code = sources[...] * (1 << plan.bits) + operators[...]
+        code = plan.place(sources[...]) * (1 << plan.bits) + operators[...]
         at = lax.broadcasted_iota(jnp.int32, code.shape, 1)
         parent = lax.broadcasted_iota(jnp.int32, code.shape, 0)
         limit = jnp.zeros(code.shape, jnp.int32)
         for p in range(parents_dev):
             limit = jnp.where(parent == p, counts[p], limit)
-        codes[...] = jnp.full(codes.shape, -1.0, F32)
-        codes[:, 0 : plan.length] = jnp.where(at < limit, code, -1).astype(F32)
+        codes[...] = jnp.full(codes.shape, plan.none, jnp.int32)
+        codes[:, 0 : plan.length] = jnp.where(at < limit, code, plan.none)
 
         first[1].wait()
         rows = coef[...].reshape(2 * boxes, coef.shape[2])
@@ -135,39 +177,44 @@
         leaf = jnp.transpose(leaf_t)[0 : 2 * boxes].astype(BF16)
 
         lane = lax.broadcasted_iota(jnp.int32, (parents_dev, 128), 1)
-        tails = {}
-        for tile, start, count, first_entry in plan.pieces:
-            turn = (start - first_entry) % plan.code_width
-            moved = codes[...] if turn == 0 else pltpu.roll(codes[...], turn, 1)
-            tails[tile] = (moved[:, 0:128], (lane >= start) & (lane < start + count))
-
-        def put(w, tile, piece):
-            for n in range(n_narrow):
-                first_row = (w * n_narrow + n) * parents_dev * plan.rows + tile
-                send[pl.ds(first_row, parents_dev, stride=plan.rows), :] = piece
+        words = plan.encode([codes[:, 128 * e : 128 * e + 128] for e in range(plan.entry_tiles)], lane)
+
+        def put(w, row, stride, piece):
+            for pair in range(plan.pairs):
+                at_row = (plan.order.index(w) * plan.pairs + pair) * plan.rows + row
+                send[pl.ds(at_row, piece.shape[0], stride=stride), :] = piece
 
         def pack(w):
             base = plan.dirs * w // 128 * 128
             shift = plan.dirs * w % 128
             span = -(-(shift + plan.dirs) // 128) * 128
             span = min(max(span, plan.width), parent_dirs - base)
+            rests = []
             for part, buf in ((0, real_buf), (1, imag_buf)):
                 value = buf[:, base : base + span]
                 if shift:
                     value = pltpu.roll(value, span - shift, 1)
-                for k in range(plan.tiles):
-                    tile = part * plan.tiles + k
-                    piece = value[:, 128 * k : 128 * k + 128]
-                    if k == plan.tiles - 1:
-                        piece = jnp.where(lane < plan.dirs - 128 * k, piece, -1.0)
-                    if tile in tails:
-                        piece = jnp.where(tails[tile][1], tails[tile][0], piece)
-                    put(w, tile, piece)
-            for e in range(plan.extra):
-                tile = 2 * plan.tiles + e
-                put(w, tile, jnp.where(tails[tile][1], tails[tile][0], -1.0))
+                for k in range(plan.full):
+                    put(w, part * plan.full + k, 2 * plan.full, value[:, 128 * k : 128 * k + 128])
+                if plan.rest:
+                    piece = value[:, 128 * plan.full : plan.width]
+                    rests.append(jnp.where(lane < plan.rest, piece, 0.0))
+            if plan.rest and plan.shared:
+                total = jnp.zeros((1, 128), F32)
+                for p in range(parents_dev):
+                    for part in range(2):
+                        turn = plan.rest_at(p, part)[1]
+                        piece = rests[part] if turn == 0 else pltpu.roll(rests[part], turn, 1)
+                        total = total + piece[p : p + 1]
+                put(w, plan.rest_row, 1, total)
+            elif plan.rest:
+                for part in range(2):
+                    put(w, plan.rest_row + part, 2, rests[part])
+            for e, word in enumerate(words):
+                put(w, plan.list_row + e, plan.list_rows, word.astype(F32))
 
         packed = 0
+        n_wide = plan.n_wide
         for c in range(n_chunks):
             copies[c].wait()
             cut = slice(cuts[c], cuts[c + 1])
@@ -186,41 +233,64 @@
     return kernel
 
 
-def translate_kernel(plan, n_wide, n_narrow, parents_dev):
-    targets = n_wide * parents_dev
+def translate_kernel(plan):
+    own = plan.own
+    targets = plan.n_wide * own
     group = max(1, min(targets, 1024 // plan.parents))
     step = min(256, plan.width)
 
-    def kernel(table_in, received, out, table, tally, a_real, a_imag):
+    def kernel(table_in, received, out, table, tally, a_real, a_imag, keys, lows):
         mine = lax.axis_index("narrow")
+        own_block = lax.rem(mine, plan.cores) * plan.peers + lax.div(mine, plan.cores)
         table[...] = jnp.zeros(table.shape, BF16)
         table[:, 0 : plan.dirs, 0 : plan.ops] = table_in[...].astype(BF16)
-        lane = lax.broadcasted_iota(jnp.int32, (1, 128), 1)
         highs = table.shape[2] // 128
         kind = BF16 if highs * plan.parents <= 256 else F32
         key_at = lax.broadcasted_iota(jnp.int32, (highs * plan.parents, 128), 0).astype(kind)
         low_at = lax.broadcasted_iota(jnp.int32, (128, 128), 0).astype(BF16)
+        lane = lax.broadcasted_iota(jnp.int32, (targets, 128), 1)
+
+        words = []
+        for e in range(plan.list_rows):
+            rows = [
+                received[
+                    pl.ds((own_block + i * plan.pairs) * plan.rows + plan.list_row + p * plan.list_rows + e, 1), :
+                ]
+                for i in range(plan.n_wide)
+                for p in range(own)
+            ]
+            words.append(jnp.concatenate(rows, 0).astype(jnp.int32))
+        for e, entry in enumerate(plan.decode(words, lane)):
+            op = entry & ((1 << plan.bits) - 1)
+            high = op >> 7
+            keys[e] = jnp.where(high < highs, high * plan.parents + (entry >> plan.bits), -1)
+            lows[e] = op & 127
+
+        def pattern(part, k):
+            pieces = []
+            for p in range(own):
+                if k < plan.full:
+                    row, turn = (2 * p + part) * plan.full + k, 0
+                else:
+                    row, turn = plan.rest_at(p, part)
+                piece = received[pl.ds(row, plan.devices, stride=plan.rows), :]
+                pieces.append(pltpu.roll(piece, 128 - turn, 1) if turn else piece)
+            return jnp.concatenate(pieces, 0)
 
         def do_group(first_target):
             for i in range(group):
-                target = first_target + i
-                w = target // parents_dev
-                p = target % parents_dev
-                row = ((w * n_narrow + mine) * parents_dev + p) * plan.rows
-                keys, lows = [], []
-                for tile, start, count, _ in plan.pieces:
-                    code = received[pl.ds(row + tile, 1), :]
-                    code = jnp.where((lane >= start) & (lane < start + count), code, -1.0).astype(jnp.int32)
-                    op = code & ((1 << plan.bits) - 1)
-                    key = jnp.where(code < 0, -1, (op >> 7) * plan.parents + (code >> plan.bits))
-                    keys.append(jnp.where(key_at == key.astype(kind), jnp.ones((), kind), jnp.zeros((), kind)).astype(BF16))
-                    lows.append(jnp.where(low_at == (op & 127).astype(BF16), jnp.ones((), BF16), jnp.zeros((), BF16)))
+                key_hits, low_hits = [], []
+                for e in range(plan.entry_tiles):
+                    key = keys[e, pl.ds(first_target + i, 1), :].astype(kind)
+                    low = lows[e, pl.ds(first_target + i, 1), :].astype(BF16)
+                    key_hits.append(jnp.where(key_at == key, jnp.ones((), kind), jnp.zeros((), kind)).astype(BF16))
+                    low_hits.append(jnp.where(low_at == low, jnp.ones((), BF16), jnp.zeros((), BF16)))
                 count_of = lax.dot_general(
-                    jnp.concatenate(keys, 1), jnp.concatenate(lows, 1), NT, preferred_element_type=F32
+                    jnp.concatenate(key_hits, 1), jnp.concatenate(low_hits, 1), NT, preferred_element_type=F32
                 ).astype(BF16)
-                own = slice(i * plan.parents, (i + 1) * plan.parents)
+                rows = slice(i * plan.parents, (i + 1) * plan.parents)
                 for h in range(highs):
-                    tally[own, 128 * h : 128 * h + 128] = count_of[h * plan.parents : (h + 1) * plan.parents]
+                    tally[rows, 128 * h : 128 * h + 128] = count_of[h * plan.parents : (h + 1) * plan.parents]
             for j in range(plan.width // step):
                 cut = slice(j * step, (j + 1) * step)
                 for a in range(0, tally.shape[0], 512):
@@ -230,12 +300,12 @@
                 for q in range(step // 128):
                     k = j * (step // 128) + q
                     lanes = slice(128 * q, 128 * q + 128)
-                    out_real = received[pl.ds(k, plan.parents, stride=plan.rows), :]
-                    out_imag = received[pl.ds(plan.tiles + k, plan.parents, stride=plan.rows), :]
+                    out_real = pattern(0, k)
+                    out_imag = pattern(1, k)
                     for i in range(group):
-                        own = slice(i * plan.parents, (i + 1) * plan.parents)
-                        op_real = a_real[own, lanes]
-                        op_imag = a_imag[own, lanes]
+                        rows = slice(i * plan.parents, (i + 1) * plan.parents)
+                        op_real = a_real[rows, lanes]
+                        op_imag = a_imag[rows, lanes]
                         real = jnp.sum(op_real * out_real - op_imag * out_imag, 0, keepdims=True)
                         imag = jnp.sum(op_real * out_imag + op_imag * out_real, 0, keepdims=True)
                         at = (first_target + i) * 2 * plan.tiles + k
@@ -250,7 +320,7 @@
     return kernel, group, step
 
 
-def downward_kernel(plan, n_wide):
+def downward_kernel(plan):
     def kernel(received, cosines, sines, interp, rad, product, inner, twin):
         parent_dirs = cosines.shape[1]
         leaf_dirs = rad.shape[0]
@@ -259,12 +329,12 @@
         parts = 2 * parents_dev
         lane = lax.broadcasted_iota(jnp.int32, (parts, plan.width), 1)
         inner[...] = jnp.zeros(inner.shape, F32)
-        for w in range(n_wide):
+        for i, w in enumerate(plan.order):
             base = plan.dirs * w // 128 * 128
             shift = plan.dirs * w % 128
             span = -(-(shift + plan.dirs) // 128) * 128
             tiles = [
-                received[pl.ds(w * parts * plan.tiles + k, parts, stride=plan.tiles), :]
+                received[pl.ds(i * parts * plan.tiles + k, parts, stride=plan.tiles), :]
                 for k in range(plan.tiles)
             ]
             value = tiles[0] if plan.tiles == 1 else jnp.concatenate(tiles, 1)
@@ -316,10 +386,9 @@
     bases = coefficients.shape[2]
     n_wide = lax.axis_size("wide")
     n_narrow = lax.axis_size("narrow")
-    n_all = n_wide * n_narrow
     dirs = translations.shape[2]
     n_ops = translations.shape[0]
-    plan = Plan(parents_dev * n_all, dirs, sources.shape[1], n_ops)
+    plan = Plan(parents_dev, n_wide, n_narrow, dirs, sources.shape[1], n_ops)
     rad = jnp.transpose(radiation, (2, 0, 1))
     table = jnp.transpose(translations, (1, 2, 0))
     cuts = [0, 1664]
@@ -328,9 +397,9 @@
     anywhere = pl.BlockSpec(memory_space=pl.ANY)
 
     send, cosines, sines = pl.pallas_call(
-        upward_kernel(plan, n_wide, n_narrow, cuts),
+        upward_kernel(plan, cuts),
         out_shape=(
-            jax.ShapeDtypeStruct((n_all * parents_dev * plan.rows, 128), F32),
+            jax.ShapeDtypeStruct((plan.peers * plan.rows, 128), F32),
             jax.ShapeDtypeStruct(angles.shape, F32),
             jax.ShapeDtypeStruct(angles.shape, F32),
         ),
@@ -346,7 +415,7 @@
             pltpu.VMEM(operators.shape, jnp.int32),
             pltpu.VMEM((2 * leaf_dirs, 128), F32),
             pltpu.VMEM((2 * leaf_dirs, 128), F32),
-            pltpu.VMEM((parents_dev, plan.code_width), F32),
+            pltpu.VMEM((parents_dev, 128 * plan.entry_tiles), jnp.int32),
             pltpu.VMEM((parents_dev, parent_dirs), F32),
             pltpu.VMEM((parents_dev, parent_dirs), F32),
             pltpu.SemaphoreType.DMA((len(cuts) + 5,)),
@@ -355,11 +424,15 @@
         name="upward",
     )(counts, coefficients, rad, interpolation, angles, sources, operators)
 
-    send = send.reshape(n_all, parents_dev * plan.rows, 128)
-    received = lax.all_to_all(send, ("wide", "narrow"), split_axis=0, concat_axis=0, tiled=True)
-    received = received.reshape(-1, 128)
-
-    body, group, step = translate_kernel(plan, n_wide, n_narrow, parents_dev)
+    send = send.reshape(plan.peers, 1, plan.rows * 128)
+    received = lax.all_to_all(
+        send, ("wide", "narrow"), split_axis=0, concat_axis=0, tiled=True, axis_index_groups=plan.groups()
+    ).reshape(-1, 128)
+    if plan.cores > 1:
+        together = [[pair * plan.cores + core for core in range(plan.cores)] for pair in range(plan.pairs)]
+        received = lax.all_gather(received, "narrow", axis=0, tiled=True, axis_index_groups=together)
+
+    body, group, step = translate_kernel(plan)
     op_lanes = -(-n_ops // 128) * 128
     incoming = pl.pallas_call(
         body,
@@ -371,17 +444,21 @@
             pltpu.VMEM((group * plan.parents, op_lanes), BF16),
             pltpu.VMEM((group * plan.parents, step), F32),
             pltpu.VMEM((group * plan.parents, step), F32),
+            pltpu.VMEM((plan.entry_tiles, n_wide * parents_dev, 128), jnp.int32),
+            pltpu.VMEM((plan.entry_tiles, n_wide * parents_dev, 128), jnp.int32),
         ],
         compiler_params=pltpu.CompilerParams(vmem_limit_bytes=24 * MIB),
         name="translate",
     )(table, received)
 
     incoming = incoming.reshape(n_wide, parents_dev * 2 * plan.tiles, 128)
-    back = lax.all_to_all(incoming, "wide", split_axis=0, concat_axis=0, tiled=True)
+    back = lax.all_to_all(
+        incoming, "wide", split_axis=0, concat_axis=0, tiled=True, axis_index_groups=[plan.order]
+    )
     back = back.reshape(-1, 128)
 
     return pl.pallas_call(
-        downward_kernel(plan, n_wide),
+        downward_kernel(plan),
         out_shape=jax.ShapeDtypeStruct((boxes, 2, bases), F32),
         in_specs=[vmem] * 5,
         out_specs=vmem,

time: 37.3 us -> 34.3 us (0.920)
  blocking collectives: 27.4 us -> 24.3 us
    all_to_all x1, blocking collectives: 17.9 us -> 14 us  [on_device(): lax.all_to_all(send, ('wide', 'narrow'), split_axis=0, concat_axis=0, til...]
    all_gather x0 -> x1, blocking collectives: none -> 1.97 us  [on_device(): lax.all_gather(received, 'narrow', axis=0, tiled=True, axis_index_groups=...]
    all_to_all x1, blocking collectives: 9.51 us -> 8.28 us  [on_device(): lax.all_to_all(incoming, 'wide', split_axis=0, concat_axis=0, tiled=True,...]
where the time goes in v4:
time: 34.3 us; the launch traced here: 34 us
  blocking collectives  24.3 us (71%)
  Pallas kernels  9.67 us (28%)
    all_to_all x1, blocking collectives, on_device(): lax.all_to_all(send, ('wide', 'narrow'), split_axis=0, concat_axis=0, til...  14 us
    all_to_all x1, blocking collectives, on_device(): lax.all_to_all(incoming, 'wide', split_axis=0, concat_axis=0, tiled=True,...  8.28 us
    pallas_call x1, Pallas kernels, on_device(): pl.pallas_call(upward_kernel(plan, cuts), out_shape=(jax.ShapeDtypeStruct...  5.03 us
    pallas_call x1, Pallas kernels, on_device(): pl.pallas_call(downward_kernel(plan), out_shape=jax.ShapeDtypeStruct((box...  2.76 us
    all_gather x1, blocking collectives, on_device(): lax.all_gather(received, 'narrow', axis=0, tiled=True, axis_index_groups=...  1.97 us
    pallas_call x1, Pallas kernels, on_device(): pl.pallas_call(body, out_shape=jax.ShapeDtypeStruct((n_wide * parents_dev...  1.88 us

profile of v4, /device:TPU:0, one launch (start us, length us, event | category | flops | bytes accessed | tf_op | source)
XLA Modules:
  0.0 34.0 jit_solution(14981973566466895483)
XLA Ops:
  0.0 0.0 copy-start.2
  0.0 0.0 copy-start
  0.0 5.0 %upward.1 = (f32[240,128]{1,0:T(8,128)}, f32[8,3328]{1,0:T(8,128)}, f32[8,3328]{1,0:T(8,128)}) custom-call(s32[2]{0:T(128)} %counts_hbm.1, bf16[16,2,512]{2,1,0:T(2,128)(2,1)} %coef_hbm.1, bf16[882,2,512]{2,1,0:T(2,128)(2,1)} %bitcast.6, bf16[882,3328]{1,0:T(8,128)(2,1)} %interp.1, f32[8,3328]{1,0:T(8,128)} %angles_hbm.1, s32[2,189]{1,0:T(2,128)} %sources_hbm.1, ...), custom_call_target="tpu_custom_call" | custom-call | tf_op jit(solution)/shard_map/upward/pallas_call | solution.py:399
  5.0 0.0 copy-start.1
  5.1 0.0 copy-start.3
  5.1 0.0 copy-start.4
  5.1 14.0 %all_to_all.10 = f32[16,1,1920]{2,1,0:T(1,128)S(1)} all-to-all(f32[16,1,1920]{2,1,0:T(1,128)} %bitcast.12), channel_id=1, replica_groups={{20,22,16,18,12,14,8,10,4,6,0,2,24,26,28,30},{21,23,17,19,13,15,9,11,5,..., dimensions={0} | all-to-all | bytes 245760 | tf_op jit(solution)/shard_map/all_to_all | solution.py:428
  19.1 2.0 %all_gather.3.received = f32[480,128]{1,0:T(8,128)S(1)} all-gather(f32[240,128]{1,0:T(8,128)S(1)} %bitcast.11), channel_id=1, replica_groups={{0,1},{2,3},{4,5},{6,7},{8,9},{10,11},{12,13},{14,15},{16,17},{18,19},{..., dimensions={0}, use_global_device_ids=true | all-gather | bytes 368640 | tf_op jit(solution)/shard_map/all_gather | solution.py:433
  21.1 0.0 copy-done.2
  21.1 1.9 %translate.1 = f32[128,128]{1,0:T(8,128)S(1)} custom-call(f32[2,416,316]{2,1,0:T(8,128)S(1)} %bitcast.8, f32[480,128]{1,0:T(8,128)S(1)} %all_gather.3.received), custom_call_target="tpu_custom_call" | custom-call | tf_op jit(solution)/shard_map/translate/pallas_call | solution.py:437
  22.9 8.3 %all_to_all.11 = f32[8,16,128]{2,1,0:T(8,128)S(1)} all-to-all(f32[8,16,128]{2,1,0:T(8,128)S(1)} %bitcast.10), channel_id=1, replica_groups={{20,16,12,8,4,0,24,28},{21,17,13,9,5,1,25,29},{22,18,14,10,6,2,26,30},{..., dimensions={0} | all-to-all | bytes 131072 | tf_op jit(solution)/shard_map/all_to_all | solution.py:455
  31.2 0.0 copy-done
  31.2 0.0 copy-done.1
  31.2 0.0 copy-done.3
  31.2 0.0 copy-done.4
  31.2 2.8 %downward.1 = f32[16,2,512]{2,1,0:T(2,128)} custom-call(f32[128,128]{1,0:T(8,128)S(1)} %bitcast.9, f32[8,3328]{1,0:T(8,128)S(1)} %copy-done.3, f32[8,3328]{1,0:T(8,128)S(1)} %copy-done.4, bf16[882,3328]{1,0:T(8,128)(2,1)S(1)} %copy-done, bf16[882,2,512]{2,1,0:T(2,128)(2,1)S(1)} %bitcast.7), custom_call_target="tpu_custom_call" | custom-call | tf_op jit(solution)/shard_map/downward/pallas_call | solution.py:460
Async XLA Ops:
  0.0 21.1 %copy-start.2 = (f32[316,2,416]{0,2,1:T(8,128)S(1)}, f32[316,2,416]{0,2,1:T(8,128)}, u32[]{:S(2)}) copy-start(f32[316,2,416]{0,2,1:T(8,128)} %param.12) | copy-start | bytes 3154948
  0.0 31.2 %copy-start = (bf16[882,3328]{1,0:T(8,128)(2,1)S(1)}, bf16[882,3328]{1,0:T(8,128)(2,1)}, u32[]{:S(2)}) copy-start(bf16[882,3328]{1,0:T(8,128)(2,1)} %interp.1) | copy-start | bytes 17611780
  5.0 26.2 %copy-start.1 = (bf16[2,512,882]{1,0,2:T(2,128)(2,1)S(1)}, bf16[2,512,882]{1,0,2:T(2,128)(2,1)}, u32[]{:S(2)}) copy-start(bf16[2,512,882]{1,0,2:T(2,128)(2,1)} %param.9) | copy-start | bytes 5419012
  5.1 26.2 %copy-start.3 = (f32[8,3328]{1,0:T(8,128)S(1)}, f32[8,3328]{1,0:T(8,128)}, u32[]{:S(2)}) copy-start(f32[8,3328]{1,0:T(8,128)} %get-tuple-element.9.cosines) | copy-start | bytes 319492
  5.1 26.2 %copy-start.4 = (f32[8,3328]{1,0:T(8,128)S(1)}, f32[8,3328]{1,0:T(8,128)}, u32[]{:S(2)}) copy-start(f32[8,3328]{1,0:T(8,128)} %get-tuple-element.10.sines) | copy-start | bytes 319492

commit v5 on v4

--- a/solution.py
+++ b/solution.py
@@ -116,8 +116,8 @@
 def upward_kernel(plan, cuts):
     def kernel(
         counts_hbm, coef_hbm, rad_hbm, interp_hbm, angles_hbm, sources_hbm, operators_hbm,
-        send, cos_out, sin_out,
-        counts, coef, rad, interp, angles, sources, operators,
+        send,
+        counts, coef, rad, interp, angles, sources, operators, cos_out, sin_out,
         even, odd, codes, real_buf, imag_buf, sems,
     ):
         parent_dirs = angles.shape[1]
@@ -233,23 +233,23 @@
     return kernel
 
 
-def translate_kernel(plan):
-    own = plan.own
-    targets = plan.n_wide * own
-    group = max(1, min(targets, 1024 // plan.parents))
-    step = min(256, plan.width)
-
-    def kernel(table_in, received, out, table, tally, a_real, a_imag, keys, lows):
+class Tally:
+    def __init__(self, plan):
+        self.plan = plan
+        self.targets = plan.n_wide * plan.own
+        self.group = max(1, min(self.targets, 1024 // plan.parents))
+        self.highs = -(-plan.ops // 128)
+        self.rows = self.group * plan.parents
+        self.shape = (self.rows, 128 * self.highs)
+        lists = pltpu.VMEM((plan.entry_tiles, self.targets, 128), jnp.int32)
+        self.scratch = [lists, lists]
+
+    def read(self, received, keys, lows):
+        plan = self.plan
         mine = lax.axis_index("narrow")
-        own_block = lax.rem(mine, plan.cores) * plan.peers + lax.div(mine, plan.cores)
-        table[...] = jnp.zeros(table.shape, BF16)
-        table[:, 0 : plan.dirs, 0 : plan.ops] = table_in[...].astype(BF16)
-        highs = table.shape[2] // 128
-        kind = BF16 if highs * plan.parents <= 256 else F32
-        key_at = lax.broadcasted_iota(jnp.int32, (highs * plan.parents, 128), 0).astype(kind)
-        low_at = lax.broadcasted_iota(jnp.int32, (128, 128), 0).astype(BF16)
-        lane = lax.broadcasted_iota(jnp.int32, (targets, 128), 1)
-
+        own_block = lax.div(mine, plan.cores)
+        flip = lax.rem(mine, plan.cores) * plan.peers
+        lane = lax.broadcasted_iota(jnp.int32, (self.targets, 128), 1)
         words = []
         for e in range(plan.list_rows):
             rows = [
@@ -257,72 +257,107 @@
                     pl.ds((own_block + i * plan.pairs) * plan.rows + plan.list_row + p * plan.list_rows + e, 1), :
                 ]
                 for i in range(plan.n_wide)
-                for p in range(own)
+                for p in range(plan.own)
             ]
             words.append(jnp.concatenate(rows, 0).astype(jnp.int32))
         for e, entry in enumerate(plan.decode(words, lane)):
             op = entry & ((1 << plan.bits) - 1)
             high = op >> 7
-            keys[e] = jnp.where(high < highs, high * plan.parents + (entry >> plan.bits), -1)
+            keys[e] = jnp.where(high < self.highs, high * plan.parents + ((entry >> plan.bits) ^ flip), -1)
             lows[e] = op & 127
+
+    def count(self, first_target, keys, lows, tally):
+        plan = self.plan
+        kind = BF16 if self.highs * plan.parents <= 256 else F32
+        key_at = lax.broadcasted_iota(jnp.int32, (self.highs * plan.parents, 128), 0).astype(kind)
+        low_at = lax.broadcasted_iota(jnp.int32, (128, 128), 0).astype(BF16)
+        for i in range(self.group):
+            key_hits, low_hits = [], []
+            for e in range(plan.entry_tiles):
+                key = keys[e, pl.ds(first_target + i, 1), :].astype(kind)
+                low = lows[e, pl.ds(first_target + i, 1), :].astype(BF16)
+                key_hits.append(jnp.where(key_at == key, jnp.ones((), kind), jnp.zeros((), kind)).astype(BF16))
+                low_hits.append(jnp.where(low_at == low, jnp.ones((), BF16), jnp.zeros((), BF16)))
+            count_of = lax.dot_general(
+                jnp.concatenate(key_hits, 1), jnp.concatenate(low_hits, 1), NT, preferred_element_type=F32
+            ).astype(BF16)
+            rows = slice(i * plan.parents, (i + 1) * plan.parents)
+            for h in range(self.highs):
+                tally[rows, 128 * h : 128 * h + 128] = count_of[h * plan.parents : (h + 1) * plan.parents]
+
+    def sum_operators(self, tally, table, a_real, a_imag):
+        for a in range(0, self.rows, 512):
+            z = min(a + 512, self.rows)
+            a_real[a:z, :] = lax.dot_general(tally[a:z, :], table[0], NT, preferred_element_type=F32)
+            a_imag[a:z, :] = lax.dot_general(tally[a:z, :], table[1], NT, preferred_element_type=F32)
+
+    def fill(self, table_in, table):
+        table[...] = jnp.zeros(table.shape, BF16)
+        table[:, 0 : self.plan.dirs, 0 : self.plan.ops] = table_in[...].astype(BF16)
+
+    def kernel(self, table_in, received, a_real, a_imag, table, tally, keys, lows):
+        self.read(received, keys, lows)
+        self.count(0, keys, lows, tally)
+        self.fill(table_in, table)
+        self.sum_operators(tally, table, a_real, a_imag)
+
+
+def translate_kernel(plan, tallies, ready):
+    group = tallies.group
+
+    def kernel(*refs):
+        if ready:
+            a_real, a_imag, *refs = refs
+            blocks = refs[: plan.cores]
+            (out,) = refs[plan.cores :]
+        else:
+            table_in, *refs = refs
+            blocks = refs[: plan.cores]
+            out, a_real, a_imag, table, tally, keys, lows = refs[plan.cores :]
+            tallies.read(blocks[0], keys, lows)
+            tallies.fill(table_in, table)
 
         def pattern(part, k):
             pieces = []
-            for p in range(own):
+            for p in range(plan.own):
                 if k < plan.full:
                     row, turn = (2 * p + part) * plan.full + k, 0
                 else:
                     row, turn = plan.rest_at(p, part)
-                piece = received[pl.ds(row, plan.devices, stride=plan.rows), :]
-                pieces.append(pltpu.roll(piece, 128 - turn, 1) if turn else piece)
+                for block in blocks:
+                    piece = block[pl.ds(row, plan.peers, stride=plan.rows), :]
+                    pieces.append(pltpu.roll(piece, 128 - turn, 1) if turn else piece)
             return jnp.concatenate(pieces, 0)
 
         def do_group(first_target):
-            for i in range(group):
-                key_hits, low_hits = [], []
-                for e in range(plan.entry_tiles):
-                    key = keys[e, pl.ds(first_target + i, 1), :].astype(kind)
-                    low = lows[e, pl.ds(first_target + i, 1), :].astype(BF16)
-                    key_hits.append(jnp.where(key_at == key, jnp.ones((), kind), jnp.zeros((), kind)).astype(BF16))
-                    low_hits.append(jnp.where(low_at == low, jnp.ones((), BF16), jnp.zeros((), BF16)))
-                count_of = lax.dot_general(
-                    jnp.concatenate(key_hits, 1), jnp.concatenate(low_hits, 1), NT, preferred_element_type=F32
-                ).astype(BF16)
-                rows = slice(i * plan.parents, (i + 1) * plan.parents)
-                for h in range(highs):
-                    tally[rows, 128 * h : 128 * h + 128] = count_of[h * plan.parents : (h + 1) * plan.parents]
-            for j in range(plan.width // step):
-                cut = slice(j * step, (j + 1) * step)
-                for a in range(0, tally.shape[0], 512):
-                    z = min(a + 512, tally.shape[0])
-                    a_real[a:z, :] = lax.dot_general(tally[a:z, :], table[0, cut, :], NT, preferred_element_type=F32)
-                    a_imag[a:z, :] = lax.dot_general(tally[a:z, :], table[1, cut, :], NT, preferred_element_type=F32)
-                for q in range(step // 128):
-                    k = j * (step // 128) + q
-                    lanes = slice(128 * q, 128 * q + 128)
-                    out_real = pattern(0, k)
-                    out_imag = pattern(1, k)
-                    for i in range(group):
-                        rows = slice(i * plan.parents, (i + 1) * plan.parents)
-                        op_real = a_real[rows, lanes]
-                        op_imag = a_imag[rows, lanes]
-                        real = jnp.sum(op_real * out_real - op_imag * out_imag, 0, keepdims=True)
-                        imag = jnp.sum(op_real * out_imag + op_imag * out_real, 0, keepdims=True)
-                        at = (first_target + i) * 2 * plan.tiles + k
-                        out[pl.ds(at, 1), :] = real
-                        out[pl.ds(at + plan.tiles, 1), :] = imag
-
-        if targets == group:
+            if not ready:
+                tallies.count(first_target, keys, lows, tally)
+                tallies.sum_operators(tally, table, a_real, a_imag)
+            for k in range(plan.tiles):
+                lanes = slice(128 * k, 128 * k + 128)
+                out_real = pattern(0, k)
+                out_imag = pattern(1, k)
+                for i in range(group):
+                    rows = slice(i * plan.parents, (i + 1) * plan.parents)
+                    op_real = a_real[rows, lanes]
+                    op_imag = a_imag[rows, lanes]
+                    real = jnp.sum(op_real * out_real - op_imag * out_imag, 0, keepdims=True)
+                    imag = jnp.sum(op_real * out_imag + op_imag * out_real, 0, keepdims=True)
+                    at = (first_target + i) * 2 * plan.tiles + k
+                    out[pl.ds(at, 1), :] = real
+                    out[pl.ds(at + plan.tiles, 1), :] = imag
+
+        if ready:
             do_group(0)
         else:
-            pl.loop(0, targets // group)(lambda g: do_group(g * group))
-
-    return kernel, group, step
+            pl.loop(0, tallies.targets // group)(lambda g: do_group(g * group))
+
+    return kernel
 
 
 def downward_kernel(plan):
-    def kernel(received, cosines, sines, interp, rad, product, inner, twin):
-        parent_dirs = cosines.shape[1]
+    def kernel(received, angles, interp, rad, product, inner, twin):
+        parent_dirs = angles.shape[1]
         leaf_dirs = rad.shape[0]
         parents_dev = product.shape[0] // 8
         boxes = product.shape[0]
@@ -345,8 +380,7 @@
                 value = pltpu.roll(value, shift, 1)
             span = min(value.shape[1], inner.shape[1] - base)
             inner[:, base : base + span] += value[:, 0:span]
-        cs = cosines[...]
-        sn = sines[...]
+        sn, cs = sin_cos(angles[...])
         reals, imags = [], []
         for p in range(parents_dev):
             in_real = inner[2 * p : 2 * p + 1, 0:parent_dirs]
@@ -396,15 +430,11 @@
     vmem = pl.BlockSpec(memory_space=pltpu.VMEM)
     anywhere = pl.BlockSpec(memory_space=pl.ANY)
 
-    send, cosines, sines = pl.pallas_call(
+    send = pl.pallas_call(
         upward_kernel(plan, cuts),
-        out_shape=(
-            jax.ShapeDtypeStruct((plan.peers * plan.rows, 128), F32),
-            jax.ShapeDtypeStruct(angles.shape, F32),
-            jax.ShapeDtypeStruct(angles.shape, F32),
-        ),
+        out_shape=jax.ShapeDtypeStruct((plan.peers * plan.rows, 128), F32),
         in_specs=[anywhere] * 7,
-        out_specs=(vmem, vmem, vmem),
+        out_specs=vmem,
         scratch_shapes=[
             pltpu.SMEM((parents_dev,), jnp.int32),
             pltpu.VMEM((boxes, 2, bases), BF16),
@@ -413,6 +443,8 @@
             pltpu.VMEM(angles.shape, F32),
             pltpu.VMEM(sources.shape, jnp.int32),
             pltpu.VMEM(operators.shape, jnp.int32),
+            pltpu.VMEM(angles.shape, F32),
+            pltpu.VMEM(angles.shape, F32),
             pltpu.VMEM((2 * leaf_dirs, 128), F32),
             pltpu.VMEM((2 * leaf_dirs, 128), F32),
             pltpu.VMEM((parents_dev, 128 * plan.entry_tiles), jnp.int32),
@@ -428,28 +460,39 @@
     received = lax.all_to_all(
         send, ("wide", "narrow"), split_axis=0, concat_axis=0, tiled=True, axis_index_groups=plan.groups()
     ).reshape(-1, 128)
+    blocks = [received]
     if plan.cores > 1:
-        together = [[pair * plan.cores + core for core in range(plan.cores)] for pair in range(plan.pairs)]
-        received = lax.all_gather(received, "narrow", axis=0, tiled=True, axis_index_groups=together)
-
-    body, group, step = translate_kernel(plan)
-    op_lanes = -(-n_ops // 128) * 128
+        blocks.append(lax.ppermute(received, "narrow", [(i, i ^ 1) for i in range(n_narrow)]))
+
+    tallies = Tally(plan)
+    ready = tallies.targets == tallies.group
+    sums = jax.ShapeDtypeStruct((tallies.rows, plan.width), F32)
+    scratch = [pltpu.VMEM((2, plan.width, tallies.shape[1]), BF16), pltpu.VMEM(tallies.shape, BF16)] + tallies.scratch
+    if ready:
+        operands = pl.pallas_call(
+            tallies.kernel,
+            out_shape=(sums, sums),
+            in_specs=[vmem, vmem],
+            out_specs=(vmem, vmem),
+            scratch_shapes=scratch,
+            cost_estimate=pl.CostEstimate(flops=10**9, bytes_accessed=10**6, transcendentals=0),
+            compiler_params=pltpu.CompilerParams(vmem_limit_bytes=16 * MIB),
+            name="operators",
+        )(table, received)
+        scratch = []
+    else:
+        operands = [table]
+        scratch = [pltpu.VMEM(sums.shape, F32), pltpu.VMEM(sums.shape, F32)] + scratch
+    operands = [*operands, *blocks]
     incoming = pl.pallas_call(
-        body,
+        translate_kernel(plan, tallies, ready),
         out_shape=jax.ShapeDtypeStruct((n_wide * parents_dev * 2 * plan.tiles, 128), F32),
-        in_specs=[vmem, vmem],
+        in_specs=[vmem] * len(operands),
         out_specs=vmem,
-        scratch_shapes=[
-            pltpu.VMEM((2, plan.width, op_lanes), BF16),
-            pltpu.VMEM((group * plan.parents, op_lanes), BF16),
-            pltpu.VMEM((group * plan.parents, step), F32),
-            pltpu.VMEM((group * plan.parents, step), F32),
-            pltpu.VMEM((plan.entry_tiles, n_wide * parents_dev, 128), jnp.int32),
-            pltpu.VMEM((plan.entry_tiles, n_wide * parents_dev, 128), jnp.int32),
-        ],
+        scratch_shapes=scratch,
         compiler_params=pltpu.CompilerParams(vmem_limit_bytes=24 * MIB),
         name="translate",
-    )(table, received)
+    )(*operands)
 
     incoming = incoming.reshape(n_wide, parents_dev * 2 * plan.tiles, 128)
     back = lax.all_to_all(
@@ -460,7 +503,7 @@
     return pl.pallas_call(
         downward_kernel(plan),
         out_shape=jax.ShapeDtypeStruct((boxes, 2, bases), F32),
-        in_specs=[vmem] * 5,
+        in_specs=[vmem] * 4,
         out_specs=vmem,
         scratch_shapes=[
             pltpu.VMEM((2 * parents_dev, parent_dirs + 128), F32),
@@ -468,7 +511,7 @@
         ],
         compiler_params=pltpu.CompilerParams(vmem_limit_bytes=32 * MIB),
         name="downward",
-    )(back, cosines, sines, interpolation, rad)
+    )(back, angles, interpolation, rad)
 
 
 def solution(mesh):

time: 34.3 us -> 32.9 us (0.959)
  blocking collectives: 24.3 us -> 22.2 us
  Pallas kernels: 9.67 us -> 10.4 us
    all_gather x1 -> x0, blocking collectives: 1.97 us -> none  [on_device(): lax.all_gather(received, 'narrow', axis=0, tiled=True, axis_index_groups=...]
    pallas_call x2 -> x3, Pallas kernels: 6.91 us -> 7.59 us  [the longest x1 5.03 us: on_device(): pl.pallas_call(upward_kernel(plan, cuts), out_shape=jax.ShapeDtypeStruct(...]
  transfers between devices with their start and end apart: 0 -> 1, of which waited for: 0 -> 0; matrix products, arithmetic and copies ran while one was open for 0% -> 0% of each run, Pallas kernels for 0% -> 6%
where the time goes in v5:
time: 32.9 us; the launch traced here: 32.6 us
  blocking collectives  22.2 us (67%)
  Pallas kernels  10.4 us (32%)
    all_to_all x1, blocking collectives, on_device(): lax.all_to_all(send, ('wide', 'narrow'), split_axis=0, concat_axis=0, til...  13.9 us
    all_to_all x1, blocking collectives, on_device(): lax.all_to_all(incoming, 'wide', split_axis=0, concat_axis=0, tiled=True,...  8.28 us
    pallas_call x1, Pallas kernels, on_device(): pl.pallas_call(upward_kernel(plan, cuts), out_shape=jax.ShapeDtypeStruct(...  5.03 us
    pallas_call x1, Pallas kernels, on_device(): pl.pallas_call(downward_kernel(plan), out_shape=jax.ShapeDtypeStruct((box...  2.77 us
    pallas_call x1, Pallas kernels, on_device(): pl.pallas_call(tallies.kernel, out_shape=(sums, sums), in_specs=[vmem, vm...  1.84 us
    pallas_call x1, Pallas kernels, on_device(): pl.pallas_call(translate_kernel(plan, tallies, ready), out_shape=jax.Shap...  0.71 us
  transfers between devices with their start and end apart: 1, of which 0 were waited for; matrix products, arithmetic and copies ran while one was open for 0% of the time, Pallas kernels for 6%

profile of v5, /device:TPU:0, one launch (start us, length us, event | category | flops | bytes accessed | tf_op | source)
XLA Modules:
  0.0 32.6 jit_solution(12149169034129911158)
XLA Ops:
  0.0 0.0 copy-start.2
  0.0 0.0 slice-start
  0.0 5.0 %upward.1 = f32[240,128]{1,0:T(8,128)} custom-call(s32[2]{0:T(128)} %counts_hbm.1, bf16[16,2,512]{2,1,0:T(2,128)(2,1)} %coef_hbm.1, bf16[882,2,512]{2,1,0:T(2,128)(2,1)} %bitcast.8, bf16[882,3328]{1,0:T(8,128)(2,1)} %interp.1, f32[8,3328]{1,0:T(8,128)} %angles.1, s32[2,189]{1,0:T(2,128)} %sources_hbm.1, s32[2,189]{1,0:T(2,128)} %operators_hbm.1), custom_call_target="tpu_custom_call" | custom-call | tf_op jit(solution)/shard_map/upward/pallas_call | solution.py:433
  5.0 13.9 %all_to_all.10 = f32[16,1,1920]{2,1,0:T(1,128)S(1)} all-to-all(f32[16,1,1920]{2,1,0:T(1,128)} %bitcast.16), channel_id=1, replica_groups={{20,22,16,18,12,14,8,10,4,6,0,2,24,26,28,30},{21,23,17,19,13,15,9,11,5,..., dimensions={0} | all-to-all | bytes 245760 | tf_op jit(solution)/shard_map/all_to_all | solution.py:460
  18.9 0.0 collective-permute-start
  18.9 0.0 copy-done.2
  18.9 0.0 slice-start.1
  18.9 1.8 %operators.1 = (f32[1024,512]{1,0:T(8,128)S(1)}, f32[1024,512]{1,0:T(8,128)S(1)}) custom-call(f32[2,416,316]{2,1,0:T(8,128)S(1)} %bitcast.15, f32[240,128]{1,0:T(8,128)S(1)} %bitcast.11), custom_call_target="tpu_custom_call" | custom-call | flops 1000000000 | bytes 1000000 | tf_op jit(solution)/shard_map/operators/pallas_call | solution.py:472
  20.8 0.0 collective-permute-done.refs_3_
  20.8 0.0 copy-start
  20.8 0.0 copy-start.1
  20.8 0.7 %translate.1 = f32[128,128]{1,0:T(8,128)S(1)} custom-call(f32[1024,512]{1,0:T(8,128)S(1)} %get-tuple-element.7.refs_0_, f32[1024,512]{1,0:T(8,128)S(1)} %get-tuple-element.8.refs_1_, f32[240,128]{1,0:T(8,128)S(1)} %bitcast.12, f32[240,128]{1,0:T(8,128)S(1)} %collective-permute-done.refs_3_), custom_call_target="tpu_custom_call" | custom-call | tf_op jit(solution)/shard_map/translate/pallas_call | solution.py:487
  21.5 8.3 %all_to_all.11 = f32[8,16,128]{2,1,0:T(8,128)S(1)} all-to-all(f32[8,16,128]{2,1,0:T(8,128)S(1)} %bitcast.13), channel_id=1, replica_groups={{20,16,12,8,4,0,24,28},{21,17,13,9,5,1,25,29},{22,18,14,10,6,2,26,30},{..., dimensions={0} | all-to-all | bytes 131072 | tf_op jit(solution)/shard_map/all_to_all | solution.py:498
  29.8 0.0 slice-done
  29.8 0.0 slice-done.1
  29.8 0.0 copy-done
  29.8 0.0 copy-done.1
  29.9 2.8 %downward.1 = f32[16,2,512]{2,1,0:T(2,128)} custom-call(f32[128,128]{1,0:T(8,128)S(1)} %bitcast.14, f32[8,3328]{1,0:T(8,128)S(1)} %copy-done.1, bf16[882,3328]{1,0:T(8,128)(2,1)S(1)} %bitcast.7, bf16[882,2,512]{2,1,0:T(2,128)(2,1)S(1)} %bitcast.9), custom_call_target="tpu_custom_call" | custom-call | tf_op jit(solution)/shard_map/downward/pallas_call | solution.py:503
  (1 shorter events, 0.0 us)
Async XLA Ops:
  0.0 18.9 %copy-start.2 = (f32[316,2,416]{0,2,1:T(8,128)S(1)}, f32[316,2,416]{0,2,1:T(8,128)}, u32[]{:S(2)}) copy-start(f32[316,2,416]{0,2,1:T(8,128)} %param.12) | copy-start | bytes 3154948
  0.0 29.8 %slice-start = ((s8[5910528]{0:T(1024)(128)(4,1)}), s8[1716224]{0:T(1024)(128)(4,1)S(1)}, s32[]{:S(2)}) async-start(s8[5910528]{0:T(1024)(128)(4,1)} %bitcast.6), calls=%async_computation.2 | async-start | bytes 3432448
  18.9 1.9 %collective-permute-start = (f32[240,128]{1,0:T(8,128)S(1)}, f32[240,128]{1,0:T(8,128)S(1)}, u32[]{:S(2)}, u32[]{:S(2)}) collective-permute-start(f32[240,128]{1,0:T(8,128)S(1)} %bitcast.10), channel_id=1, source_target_pairs={{0,1},{1,0},{2,3},{3,2},{4,5},{5,4},{6,7},{7,6},{8,9},{9,8},{10,11... | collective-permute-start | bytes 368648 | tf_op jit(solution)/shard_map/ppermute | solution.py:465
  18.9 10.9 %slice-start.1 = ((s8[5910528]{0:T(1024)(128)(4,1)}), s8[4194304]{0:T(1024)(128)(4,1)S(1)}, s32[]{:S(2)}) async-start(s8[5910528]{0:T(1024)(128)(4,1)} %bitcast.6), calls=%async_computation.3 | async-start | bytes 8388608
  20.8 9.0 %copy-start = (bf16[2,512,882]{1,0,2:T(2,128)(2,1)S(1)}, bf16[2,512,882]{1,0,2:T(2,128)(2,1)}, u32[]{:S(2)}) copy-start(bf16[2,512,882]{1,0,2:T(2,128)(2,1)} %param.9) | copy-start | bytes 5419012
  20.8 9.0 %copy-start.1 = (f32[8,3328]{1,0:T(8,128)S(1)}, f32[8,3328]{1,0:T(8,128)}, u32[]{:S(2)}) copy-start(f32[8,3328]{1,0:T(8,128)} %angles.1) | copy-start | bytes 319492

commit v6 on v5

--- a/solution.py
+++ b/solution.py
@@ -47,10 +47,23 @@
             return self.rest_row, (2 * p + part) * self.rest
         return self.rest_row + 2 * p + part, 0
 
+    def swap(self, w, pair):
+        return w // (self.n_wide // 2) if self.cores > 1 else 0
+
+    def device(self, w, pair, label):
+        return w * self.n_narrow + pair * self.cores + (label ^ self.swap(w, pair))
+
     def groups(self):
         return [
-            [w * self.n_narrow + pair * self.cores + core for w in self.order for pair in range(self.pairs)]
-            for core in range(self.cores)
+            [self.device(w, pair, label) for w in self.order for pair in range(self.pairs)]
+            for label in range(self.cores)
+        ]
+
+    def wide_groups(self):
+        return [
+            [self.device(w, pair, label) for w in self.order]
+            for pair in range(self.pairs)
+            for label in range(self.cores)
         ]
 
     def place(self, source):
@@ -59,10 +72,9 @@
         place = jnp.zeros(source.shape, jnp.int32)
         for i, w in enumerate(self.order):
             for pair in range(self.pairs):
-                for core in range(self.cores):
-                    flat = w * self.n_narrow + pair * self.cores + core
-                    block = core * self.peers + i * self.pairs + pair
-                    place = jnp.where(device == flat, block, place)
+                for label in range(self.cores):
+                    block = label * self.peers + i * self.pairs + pair
+                    place = jnp.where(device == self.device(w, pair, label), block, place)
         return (source & (self.own - 1)) * self.devices + place
 
     def encode(self, entries, lane):
@@ -118,7 +130,7 @@
         counts_hbm, coef_hbm, rad_hbm, interp_hbm, angles_hbm, sources_hbm, operators_hbm,
         send,
         counts, coef, rad, interp, angles, sources, operators, cos_out, sin_out,
-        even, odd, codes, real_buf, imag_buf, sems,
+        even, odd, codes, out_buf, sems,
     ):
         parent_dirs = angles.shape[1]
         leaf_dirs = rad.shape[0]
@@ -184,51 +196,48 @@
                 at_row = (plan.order.index(w) * plan.pairs + pair) * plan.rows + row
                 send[pl.ds(at_row, piece.shape[0], stride=stride), :] = piece
 
+        for w in range(plan.n_wide):
+            for e, word in enumerate(words):
+                put(w, plan.list_row + e, plan.list_rows, word.astype(F32))
+
+        wide_lane = lax.broadcasted_iota(jnp.int32, (2 * parents_dev, 128), 1)
+
         def pack(w):
             base = plan.dirs * w // 128 * 128
             shift = plan.dirs * w % 128
             span = -(-(shift + plan.dirs) // 128) * 128
             span = min(max(span, plan.width), parent_dirs - base)
-            rests = []
-            for part, buf in ((0, real_buf), (1, imag_buf)):
-                value = buf[:, base : base + span]
-                if shift:
-                    value = pltpu.roll(value, span - shift, 1)
-                for k in range(plan.full):
-                    put(w, part * plan.full + k, 2 * plan.full, value[:, 128 * k : 128 * k + 128])
-                if plan.rest:
-                    piece = value[:, 128 * plan.full : plan.width]
-                    rests.append(jnp.where(lane < plan.rest, piece, 0.0))
-            if plan.rest and plan.shared:
-                total = jnp.zeros((1, 128), F32)
-                for p in range(parents_dev):
-                    for part in range(2):
-                        turn = plan.rest_at(p, part)[1]
-                        piece = rests[part] if turn == 0 else pltpu.roll(rests[part], turn, 1)
-                        total = total + piece[p : p + 1]
-                put(w, plan.rest_row, 1, total)
-            elif plan.rest:
-                for part in range(2):
-                    put(w, plan.rest_row + part, 2, rests[part])
-            for e, word in enumerate(words):
-                put(w, plan.list_row + e, plan.list_rows, word.astype(F32))
-
-        packed = 0
+            value = out_buf[:, base : base + span]
+            if shift:
+                value = pltpu.roll(value, span - shift, 1)
+            for k in range(plan.full):
+                put(w, k, plan.full, value[:, 128 * k : 128 * k + 128])
+            if plan.rest:
+                piece = jnp.where(wide_lane < plan.rest, value[:, 128 * plan.full : plan.width], 0.0)
+                if plan.shared:
+                    piece = sum(
+                        pltpu.roll(piece[r : r + 1], plan.rest * r, 1) if r else piece[0:1]
+                        for r in range(2 * parents_dev)
+                    )
+                put(w, plan.rest_row, 1, piece)
+
         n_wide = plan.n_wide
+        ups = []
         for c in range(n_chunks):
             copies[c].wait()
+            ups.append(jnp.dot(leaf, interp[:, cuts[c] : cuts[c + 1]], preferred_element_type=F32))
+        for c in range(n_chunks):
             cut = slice(cuts[c], cuts[c + 1])
-            up = jnp.dot(leaf, interp[:, cut], preferred_element_type=F32)
+            up = ups[c]
             cs = cos_out[:, cut]
             sn = sin_out[:, cut]
             for p in range(parents_dev):
                 up_real = up[8 * p : 8 * p + 8]
                 up_imag = up[boxes + 8 * p : boxes + 8 * p + 8]
-                real_buf[p : p + 1, cut] = jnp.sum(cs * up_real - sn * up_imag, 0, keepdims=True)
-                imag_buf[p : p + 1, cut] = jnp.sum(cs * up_imag + sn * up_real, 0, keepdims=True)
-            while packed < n_wide and -(-plan.dirs * (packed + 1) // 128) * 128 <= cuts[c + 1]:
-                pack(packed)
-                packed += 1
+                out_buf[2 * p : 2 * p + 1, cut] = jnp.sum(cs * up_real - sn * up_imag, 0, keepdims=True)
+                out_buf[2 * p + 1 : 2 * p + 2, cut] = jnp.sum(cs * up_imag + sn * up_real, 0, keepdims=True)
+        for w in range(n_wide):
+            pack(w)
 
     return kernel
 
@@ -248,7 +257,8 @@
         plan = self.plan
         mine = lax.axis_index("narrow")
         own_block = lax.div(mine, plan.cores)
-        flip = lax.rem(mine, plan.cores) * plan.peers
+        label = lax.rem(mine, plan.cores) ^ plan.swap(lax.axis_index("wide"), own_block)
+        flip = label * plan.peers
         lane = lax.broadcasted_iota(jnp.int32, (self.targets, 128), 1)
         words = []
         for e in range(plan.list_rows):
@@ -425,7 +435,7 @@
     plan = Plan(parents_dev, n_wide, n_narrow, dirs, sources.shape[1], n_ops)
     rad = jnp.transpose(radiation, (2, 0, 1))
     table = jnp.transpose(translations, (1, 2, 0))
-    cuts = [0, 1664]
+    cuts = [0, 1280, 2432]
     cuts = [c for c in cuts if c < parent_dirs] + [parent_dirs]
     vmem = pl.BlockSpec(memory_space=pltpu.VMEM)
     anywhere = pl.BlockSpec(memory_space=pl.ANY)
@@ -448,8 +458,7 @@
             pltpu.VMEM((2 * leaf_dirs, 128), F32),
             pltpu.VMEM((2 * leaf_dirs, 128), F32),
             pltpu.VMEM((parents_dev, 128 * plan.entry_tiles), jnp.int32),
-            pltpu.VMEM((parents_dev, parent_dirs), F32),
-            pltpu.VMEM((parents_dev, parent_dirs), F32),
+            pltpu.VMEM((2 * parents_dev, parent_dirs), F32),
             pltpu.SemaphoreType.DMA((len(cuts) + 5,)),
         ],
         compiler_params=pltpu.CompilerParams(vmem_limit_bytes=56 * MIB),
@@ -496,7 +505,7 @@
 
     incoming = incoming.reshape(n_wide, parents_dev * 2 * plan.tiles, 128)
     back = lax.all_to_all(
-        incoming, "wide", split_axis=0, concat_axis=0, tiled=True, axis_index_groups=[plan.order]
+        incoming, ("wide", "narrow"), split_axis=0, concat_axis=0, tiled=True, axis_index_groups=plan.wide_groups()
     )
     back = back.reshape(-1, 128)
 

time: 32.9 us -> 31.8 us (0.967)
  blocking collectives: 22.2 us -> 20.2 us
  starting transfers between devices: 0.01 us -> 1.14 us
    all_to_all x1, blocking collectives: 13.9 us -> 12.6 us  [on_device(): lax.all_to_all(send, ('wide', 'narrow'), split_axis=0, concat_axis=0, til...]
    ppermute x1, starting transfers between devices: 0.01 us -> 1.14 us  [on_device(): lax.ppermute(received, 'narrow', [(i, i ^ 1) for i in range(n_narrow)])]
    all_to_all x1, blocking collectives: 8.28 us -> 7.59 us  [on_device(): lax.all_to_all(incoming, ('wide', 'narrow'), split_axis=0, concat_axis=0,...]
where the time goes in v6:
time: 31.8 us; the launch traced here: 31.6 us
  blocking collectives  20.2 us (64%)
  Pallas kernels  10.2 us (32%)
  starting transfers between devices  1.14 us (4%)
    all_to_all x1, blocking collectives, on_device(): lax.all_to_all(send, ('wide', 'narrow'), split_axis=0, concat_axis=0, til...  12.6 us
    all_to_all x1, blocking collectives, on_device(): lax.all_to_all(incoming, ('wide', 'narrow'), split_axis=0, concat_axis=0,...  7.59 us
    pallas_call x1, Pallas kernels, on_device(): pl.pallas_call(upward_kernel(plan, cuts), out_shape=jax.ShapeDtypeStruct(...  4.9 us
    pallas_call x1, Pallas kernels, on_device(): pl.pallas_call(downward_kernel(plan), out_shape=jax.ShapeDtypeStruct((box...  2.76 us
    pallas_call x1, Pallas kernels, on_device(): pl.pallas_call(tallies.kernel, out_shape=(sums, sums), in_specs=[vmem, vm...  1.83 us
    ppermute x1, starting transfers between devices, on_device(): lax.ppermute(received, 'narrow', [(i, i ^ 1) for i in range(n_narrow)])  1.14 us
    pallas_call x1, Pallas kernels, on_device(): pl.pallas_call(translate_kernel(plan, tallies, ready), out_shape=jax.Shap...  0.71 us
  transfers between devices with their start and end apart: 1, of which 0 were waited for; matrix products, arithmetic and copies ran while one was open for 0% of the time, Pallas kernels for 6%

profile of v6, /device:TPU:0, one launch (start us, length us, event | category | flops | bytes accessed | tf_op | source)
XLA Modules:
  0.0 31.6 jit_solution(600384430346457106)
XLA Ops:
  0.0 0.0 copy-start.2
  0.0 0.0 slice-start
  0.0 4.9 %upward.1 = f32[240,128]{1,0:T(8,128)} custom-call(s32[2]{0:T(128)} %counts_hbm.1, bf16[16,2,512]{2,1,0:T(2,128)(2,1)} %coef_hbm.1, bf16[882,2,512]{2,1,0:T(2,128)(2,1)} %bitcast.8, bf16[882,3328]{1,0:T(8,128)(2,1)} %interp.1, f32[8,3328]{1,0:T(8,128)} %angles.1, s32[2,189]{1,0:T(2,128)} %sources_hbm.1, s32[2,189]{1,0:T(2,128)} %operators_hbm.1), custom_call_target="tpu_custom_call" | custom-call | tf_op jit(solution)/shard_map/upward/pallas_call | solution.py:443
  4.9 12.6 %all_to_all.10 = f32[16,1,1920]{2,1,0:T(1,128)S(1)} all-to-all(f32[16,1,1920]{2,1,0:T(1,128)} %bitcast.16), channel_id=1, replica_groups={{21,23,17,19,12,14,8,10,4,6,0,2,25,27,29,31},{20,22,16,18,13,15,9,11,5,..., dimensions={0} | all-to-all | bytes 245760 | tf_op jit(solution)/shard_map/all_to_all | solution.py:469
  17.5 1.1 %collective-permute-start = (f32[240,128]{1,0:T(8,128)S(1)}, f32[240,128]{1,0:T(8,128)S(1)}, u32[]{:S(2)}, u32[]{:S(2)}) collective-permute-start(f32[240,128]{1,0:T(8,128)S(1)} %bitcast.10), channel_id=1, source_target_pairs={{0,1},{1,0},{2,3},{3,2},{4,5},{5,4},{6,7},{7,6},{8,9},{9,8},{10,11... | collective-permute-start | bytes 368648 | tf_op jit(solution)/shard_map/ppermute | solution.py:474
  18.6 0.0 copy-done.2
  18.6 0.0 slice-start.1
  18.6 1.8 %operators.1 = (f32[1024,512]{1,0:T(8,128)S(1)}, f32[1024,512]{1,0:T(8,128)S(1)}) custom-call(f32[2,416,316]{2,1,0:T(8,128)S(1)} %bitcast.15, f32[240,128]{1,0:T(8,128)S(1)} %bitcast.11), custom_call_target="tpu_custom_call" | custom-call | flops 1000000000 | bytes 1000000 | tf_op jit(solution)/shard_map/operators/pallas_call | solution.py:481
  20.5 0.0 collective-permute-done.refs_3_
  20.5 0.0 copy-start
  20.5 0.0 copy-start.1
  20.5 0.7 %translate.1 = f32[128,128]{1,0:T(8,128)S(1)} custom-call(f32[1024,512]{1,0:T(8,128)S(1)} %get-tuple-element.7.refs_0_, f32[1024,512]{1,0:T(8,128)S(1)} %get-tuple-element.8.refs_1_, f32[240,128]{1,0:T(8,128)S(1)} %bitcast.12, f32[240,128]{1,0:T(8,128)S(1)} %collective-permute-done.refs_3_), custom_call_target="tpu_custom_call" | custom-call | tf_op jit(solution)/shard_map/translate/pallas_call | solution.py:496
  21.2 7.6 %all_to_all.11 = f32[8,16,128]{2,1,0:T(8,128)S(1)} all-to-all(f32[8,16,128]{2,1,0:T(8,128)S(1)} %bitcast.13), channel_id=1, replica_groups={{21,17,12,8,4,0,25,29},{20,16,13,9,5,1,24,28},{23,19,14,10,6,2,27,31},{..., dimensions={0} | all-to-all | bytes 131072 | tf_op jit(solution)/shard_map/all_to_all | solution.py:507
  28.8 0.0 slice-done
  28.8 0.0 slice-done.1
  28.8 0.0 copy-done
  28.8 0.0 copy-done.1
  28.8 2.8 %downward.1 = f32[16,2,512]{2,1,0:T(2,128)} custom-call(f32[128,128]{1,0:T(8,128)S(1)} %bitcast.14, f32[8,3328]{1,0:T(8,128)S(1)} %copy-done.1, bf16[882,3328]{1,0:T(8,128)(2,1)S(1)} %bitcast.7, bf16[882,2,512]{2,1,0:T(2,128)(2,1)S(1)} %bitcast.9), custom_call_target="tpu_custom_call" | custom-call | tf_op jit(solution)/shard_map/downward/pallas_call | solution.py:512
  (1 shorter events, 0.0 us)
Async XLA Ops:
  0.0 18.6 %copy-start.2 = (f32[316,2,416]{0,2,1:T(8,128)S(1)}, f32[316,2,416]{0,2,1:T(8,128)}, u32[]{:S(2)}) copy-start(f32[316,2,416]{0,2,1:T(8,128)} %param.12) | copy-start | bytes 3154948
  0.0 28.8 %slice-start = ((s8[5910528]{0:T(1024)(128)(4,1)}), s8[1716224]{0:T(1024)(128)(4,1)S(1)}, s32[]{:S(2)}) async-start(s8[5910528]{0:T(1024)(128)(4,1)} %bitcast.6), calls=%async_computation.2 | async-start | bytes 3432448
  17.5 3.0 %collective-permute-start = (f32[240,128]{1,0:T(8,128)S(1)}, f32[240,128]{1,0:T(8,128)S(1)}, u32[]{:S(2)}, u32[]{:S(2)}) collective-permute-start(f32[240,128]{1,0:T(8,128)S(1)} %bitcast.10), channel_id=1, source_target_pairs={{0,1},{1,0},{2,3},{3,2},{4,5},{5,4},{6,7},{7,6},{8,9},{9,8},{10,11... | collective-permute-start | bytes 368648 | tf_op jit(solution)/shard_map/ppermute | solution.py:474
  18.6 10.2 %slice-start.1 = ((s8[5910528]{0:T(1024)(128)(4,1)}), s8[4194304]{0:T(1024)(128)(4,1)S(1)}, s32[]{:S(2)}) async-start(s8[5910528]{0:T(1024)(128)(4,1)} %bitcast.6), calls=%async_computation.3 | async-start | bytes 8388608
  20.5 8.3 %copy-start = (bf16[2,512,882]{1,0,2:T(2,128)(2,1)S(1)}, bf16[2,512,882]{1,0,2:T(2,128)(2,1)}, u32[]{:S(2)}) copy-start(bf16[2,512,882]{1,0,2:T(2,128)(2,1)} %param.9) | copy-start | bytes 5419012
  20.5 8.3 %copy-start.1 = (f32[8,3328]{1,0:T(8,128)S(1)}, f32[8,3328]{1,0:T(8,128)}, u32[]{:S(2)}) copy-start(f32[8,3328]{1,0:T(8,128)} %angles.1) | copy-start | bytes 319492

commit v7 on v6

--- a/solution.py
+++ b/solution.py
@@ -128,12 +128,12 @@
 def upward_kernel(plan, cuts):
     def kernel(
         counts_hbm, coef_hbm, rad_hbm, interp_hbm, angles_hbm, sources_hbm, operators_hbm,
-        send,
-        counts, coef, rad, interp, angles, sources, operators, cos_out, sin_out,
+        send_out,
+        send, counts, coef, rad, interp, angles, sources, operators, cos_out, sin_out,
         even, odd, codes, out_buf, sems,
     ):
         parent_dirs = angles.shape[1]
-        leaf_dirs = rad.shape[0]
+        leaf_dirs = rad_hbm.shape[0]
         boxes = coef.shape[0]
         parents_dev = boxes // 8
         n_chunks = len(cuts) - 1
@@ -142,7 +142,7 @@
         for source, target in (
             (angles_hbm, angles),
             (coef_hbm, coef),
-            (rad_hbm, rad),
+            (rad_hbm, rad.at[pl.ds(0, leaf_dirs)]),
             (sources_hbm, sources),
             (operators_hbm, operators),
             (counts_hbm, counts),
@@ -178,7 +178,7 @@
         weights = jnp.concatenate([plain, turned], 0)
 
         first[2].wait()
-        matrix = rad[...].reshape(2 * leaf_dirs, rad.shape[2])
+        matrix = rad[0:leaf_dirs].reshape(2 * leaf_dirs, rad.shape[2])
         weights_t = jnp.transpose(weights)
         for a in range(0, 2 * leaf_dirs, half):
             z = min(a + half, 2 * leaf_dirs)
@@ -238,6 +238,7 @@
                 out_buf[2 * p + 1 : 2 * p + 2, cut] = jnp.sum(cs * up_imag + sn * up_real, 0, keepdims=True)
         for w in range(n_wide):
             pack(w)
+        send_out[...] = send[0 : send_out.shape[0], :]
 
     return kernel
 
@@ -366,13 +367,14 @@
 
 
 def downward_kernel(plan):
-    def kernel(received, angles, interp, rad, product, inner, twin):
+    def kernel(arrived, angles, interp, rad, product, received, inner, twin):
         parent_dirs = angles.shape[1]
         leaf_dirs = rad.shape[0]
         parents_dev = product.shape[0] // 8
         boxes = product.shape[0]
         parts = 2 * parents_dev
         lane = lax.broadcasted_iota(jnp.int32, (parts, plan.width), 1)
+        received[0 : arrived.shape[0], :] = arrived[...]
         inner[...] = jnp.zeros(inner.shape, F32)
         for i, w in enumerate(plan.order):
             base = plan.dirs * w // 128 * 128
@@ -412,7 +414,7 @@
         )
         twin[pl.ds(0, leaf_dirs, stride=2), :] = got[:, 0:128]
         twin[pl.ds(1, leaf_dirs, stride=2), :] = got[:, 128:256]
-        flat = jnp.transpose(twin[...])[0 : 2 * boxes].astype(BF16)
+        flat = jnp.transpose(twin[0 : 2 * leaf_dirs, :])[0 : 2 * boxes].astype(BF16)
         matrix = rad[...].reshape(2 * leaf_dirs, rad.shape[2])
         result = jnp.dot(flat, matrix, preferred_element_type=F32)
         product[:, 0, :] = result[0:boxes]
@@ -435,6 +437,7 @@
     plan = Plan(parents_dev, n_wide, n_narrow, dirs, sources.shape[1], n_ops)
     rad = jnp.transpose(radiation, (2, 0, 1))
     table = jnp.transpose(translations, (1, 2, 0))
+    room = -(-leaf_dirs // 16) * 16 + 16
     cuts = [0, 1280, 2432]
     cuts = [c for c in cuts if c < parent_dirs] + [parent_dirs]
     vmem = pl.BlockSpec(memory_space=pltpu.VMEM)
@@ -446,17 +449,18 @@
         in_specs=[anywhere] * 7,
         out_specs=vmem,
         scratch_shapes=[
+            pltpu.VMEM((plan.peers * plan.rows + 64, 128), F32),
             pltpu.SMEM((parents_dev,), jnp.int32),
             pltpu.VMEM((boxes, 2, bases), BF16),
-            pltpu.VMEM((leaf_dirs, 2, bases), BF16),
+            pltpu.VMEM((room, 2, bases), BF16),
             pltpu.VMEM((leaf_dirs, parent_dirs), BF16),
             pltpu.VMEM(angles.shape, F32),
             pltpu.VMEM(sources.shape, jnp.int32),
             pltpu.VMEM(operators.shape, jnp.int32),
             pltpu.VMEM(angles.shape, F32),
             pltpu.VMEM(angles.shape, F32),
-            pltpu.VMEM((2 * leaf_dirs, 128), F32),
-            pltpu.VMEM((2 * leaf_dirs, 128), F32),
+            pltpu.VMEM((2 * room, 128), F32),
+            pltpu.VMEM((2 * room, 128), F32),
             pltpu.VMEM((parents_dev, 128 * plan.entry_tiles), jnp.int32),
             pltpu.VMEM((2 * parents_dev, parent_dirs), F32),
             pltpu.SemaphoreType.DMA((len(cuts) + 5,)),
@@ -515,8 +519,9 @@
         in_specs=[vmem] * 4,
         out_specs=vmem,
         scratch_shapes=[
+            pltpu.VMEM((n_wide * parents_dev * 2 * plan.tiles + 64, 128), F32),
             pltpu.VMEM((2 * parents_dev, parent_dirs + 128), F32),
-            pltpu.VMEM((2 * leaf_dirs, 128), F32),
+            pltpu.VMEM((2 * room, 128), F32),
         ],
         compiler_params=pltpu.CompilerParams(vmem_limit_bytes=32 * MIB),
         name="downward",

time: 31.8 us -> 31.9 us (level)
  no operation moved by 1% of the time
where the time goes in v7:
time: 31.9 us; the launch traced here: 31.6 us
  blocking collectives  20.2 us (63%)
  Pallas kernels  10.2 us (32%)
  starting transfers between devices  1.14 us (4%)
    all_to_all x1, blocking collectives, on_device(): lax.all_to_all(send, ('wide', 'narrow'), split_axis=0, concat_axis=0, til...  12.6 us
    all_to_all x1, blocking collectives, on_device(): lax.all_to_all(incoming, ('wide', 'narrow'), split_axis=0, concat_axis=0,...  7.6 us
    pallas_call x1, Pallas kernels, on_device(): pl.pallas_call(upward_kernel(plan, cuts), out_shape=jax.ShapeDtypeStruct(...  4.91 us
    pallas_call x1, Pallas kernels, on_device(): pl.pallas_call(downward_kernel(plan), out_shape=jax.ShapeDtypeStruct((box...  2.76 us
    pallas_call x1, Pallas kernels, on_device(): pl.pallas_call(tallies.kernel, out_shape=(sums, sums), in_specs=[vmem, vm...  1.83 us
    ppermute x1, starting transfers between devices, on_device(): lax.ppermute(received, 'narrow', [(i, i ^ 1) for i in range(n_narrow)])  1.14 us
    pallas_call x1, Pallas kernels, on_device(): pl.pallas_call(translate_kernel(plan, tallies, ready), out_shape=jax.Shap...  0.71 us
  transfers between devices with their start and end apart: 1, of which 0 were waited for; matrix products, arithmetic and copies ran while one was open for 0% of the time, Pallas kernels for 6%

profile of v7, /device:TPU:0, one launch (start us, length us, event | category | flops | bytes accessed | tf_op | source)
XLA Modules:
  0.0 31.6 jit_solution(9855065119297083646)
XLA Ops:
  0.0 0.0 copy-start.2
  0.0 0.0 slice-start
  0.0 4.9 %upward.1 = f32[240,128]{1,0:T(8,128)} custom-call(s32[2]{0:T(128)} %counts_hbm.1, bf16[16,2,512]{2,1,0:T(2,128)(2,1)} %coef_hbm.1, bf16[882,2,512]{2,1,0:T(2,128)(2,1)} %bitcast.8, bf16[882,3328]{1,0:T(8,128)(2,1)} %interp.1, f32[8,3328]{1,0:T(8,128)} %angles.1, s32[2,189]{1,0:T(2,128)} %sources_hbm.1, s32[2,189]{1,0:T(2,128)} %operators_hbm.1), custom_call_target="tpu_custom_call" | custom-call | tf_op jit(solution)/shard_map/upward/pallas_call | solution.py:446
  4.9 12.6 %all_to_all.10 = f32[16,1,1920]{2,1,0:T(1,128)S(1)} all-to-all(f32[16,1,1920]{2,1,0:T(1,128)} %bitcast.16), channel_id=1, replica_groups={{21,23,17,19,12,14,8,10,4,6,0,2,25,27,29,31},{20,22,16,18,13,15,9,11,5,..., dimensions={0} | all-to-all | bytes 245760 | tf_op jit(solution)/shard_map/all_to_all | solution.py:473
  17.5 1.1 %collective-permute-start = (f32[240,128]{1,0:T(8,128)S(1)}, f32[240,128]{1,0:T(8,128)S(1)}, u32[]{:S(2)}, u32[]{:S(2)}) collective-permute-start(f32[240,128]{1,0:T(8,128)S(1)} %bitcast.10), channel_id=1, source_target_pairs={{0,1},{1,0},{2,3},{3,2},{4,5},{5,4},{6,7},{7,6},{8,9},{9,8},{10,11... | collective-permute-start | bytes 368648 | tf_op jit(solution)/shard_map/ppermute | solution.py:478
  18.6 0.0 copy-done.2
  18.6 0.0 slice-start.1
  18.6 1.8 %operators.1 = (f32[1024,512]{1,0:T(8,128)S(1)}, f32[1024,512]{1,0:T(8,128)S(1)}) custom-call(f32[2,416,316]{2,1,0:T(8,128)S(1)} %bitcast.15, f32[240,128]{1,0:T(8,128)S(1)} %bitcast.11), custom_call_target="tpu_custom_call" | custom-call | flops 1000000000 | bytes 1000000 | tf_op jit(solution)/shard_map/operators/pallas_call | solution.py:485
  20.5 0.0 collective-permute-done.refs_3_
  20.5 0.0 copy-start
  20.5 0.0 copy-start.1
  20.5 0.7 %translate.1 = f32[128,128]{1,0:T(8,128)S(1)} custom-call(f32[1024,512]{1,0:T(8,128)S(1)} %get-tuple-element.7.refs_0_, f32[1024,512]{1,0:T(8,128)S(1)} %get-tuple-element.8.refs_1_, f32[240,128]{1,0:T(8,128)S(1)} %bitcast.12, f32[240,128]{1,0:T(8,128)S(1)} %collective-permute-done.refs_3_), custom_call_target="tpu_custom_call" | custom-call | tf_op jit(solution)/shard_map/translate/pallas_call | solution.py:500
  21.2 7.6 %all_to_all.11 = f32[8,16,128]{2,1,0:T(8,128)S(1)} all-to-all(f32[8,16,128]{2,1,0:T(8,128)S(1)} %bitcast.13), channel_id=1, replica_groups={{21,17,12,8,4,0,25,29},{20,16,13,9,5,1,24,28},{23,19,14,10,6,2,27,31},{..., dimensions={0} | all-to-all | bytes 131072 | tf_op jit(solution)/shard_map/all_to_all | solution.py:511
  28.8 0.0 slice-done
  28.8 0.0 slice-done.1
  28.8 0.0 copy-done
  28.8 0.0 copy-done.1
  28.9 2.8 %downward.1 = f32[16,2,512]{2,1,0:T(2,128)} custom-call(f32[128,128]{1,0:T(8,128)S(1)} %bitcast.14, f32[8,3328]{1,0:T(8,128)S(1)} %copy-done.1, bf16[882,3328]{1,0:T(8,128)(2,1)S(1)} %bitcast.7, bf16[882,2,512]{2,1,0:T(2,128)(2,1)S(1)} %bitcast.9), custom_call_target="tpu_custom_call" | custom-call | tf_op jit(solution)/shard_map/downward/pallas_call | solution.py:516
  (1 shorter events, 0.0 us)
Async XLA Ops:
  0.0 18.6 %copy-start.2 = (f32[316,2,416]{0,2,1:T(8,128)S(1)}, f32[316,2,416]{0,2,1:T(8,128)}, u32[]{:S(2)}) copy-start(f32[316,2,416]{0,2,1:T(8,128)} %param.12) | copy-start | bytes 3154948
  0.0 28.8 %slice-start = ((s8[5910528]{0:T(1024)(128)(4,1)}), s8[1716224]{0:T(1024)(128)(4,1)S(1)}, s32[]{:S(2)}) async-start(s8[5910528]{0:T(1024)(128)(4,1)} %bitcast.6), calls=%async_computation.2 | async-start | bytes 3432448
  17.5 3.0 %collective-permute-start = (f32[240,128]{1,0:T(8,128)S(1)}, f32[240,128]{1,0:T(8,128)S(1)}, u32[]{:S(2)}, u32[]{:S(2)}) collective-permute-start(f32[240,128]{1,0:T(8,128)S(1)} %bitcast.10), channel_id=1, source_target_pairs={{0,1},{1,0},{2,3},{3,2},{4,5},{5,4},{6,7},{7,6},{8,9},{9,8},{10,11... | collective-permute-start | bytes 368648 | tf_op jit(solution)/shard_map/ppermute | solution.py:478
  18.6 10.2 %slice-start.1 = ((s8[5910528]{0:T(1024)(128)(4,1)}), s8[4194304]{0:T(1024)(128)(4,1)S(1)}, s32[]{:S(2)}) async-start(s8[5910528]{0:T(1024)(128)(4,1)} %bitcast.6), calls=%async_computation.3 | async-start | bytes 8388608
  20.5 8.4 %copy-start = (bf16[2,512,882]{1,0,2:T(2,128)(2,1)S(1)}, bf16[2,512,882]{1,0,2:T(2,128)(2,1)}, u32[]{:S(2)}) copy-start(bf16[2,512,882]{1,0,2:T(2,128)(2,1)} %param.9) | copy-start | bytes 5419012
  20.5 8.3 %copy-start.1 = (f32[8,3328]{1,0:T(8,128)S(1)}, f32[8,3328]{1,0:T(8,128)}, u32[]{:S(2)}) copy-start(f32[8,3328]{1,0:T(8,128)} %angles.1) | copy-start | bytes 319492

commit v8 on v7

--- a/solution.py
+++ b/solution.py
@@ -306,11 +306,39 @@
         table[...] = jnp.zeros(table.shape, BF16)
         table[:, 0 : self.plan.dirs, 0 : self.plan.ops] = table_in[...].astype(BF16)
 
-    def kernel(self, table_in, received, a_real, a_imag, table, tally, keys, lows):
+    def apply(self, blocks, first_block, a_real, a_imag, targets, k):
+        plan = self.plan
+        many = len(blocks) * plan.peers
+        out = [[], []]
+        for part in range(2):
+            for p in range(plan.own):
+                row, turn = plan.rest_at(p, part) if k >= plan.full else ((2 * p + part) * plan.full + k, 0)
+                for block in blocks:
+                    piece = block[pl.ds(row, plan.peers, stride=plan.rows), :]
+                    out[part].append(pltpu.roll(piece, 128 - turn, 1) if turn else piece)
+        out_real, out_imag = [jnp.concatenate(pieces, 0) for pieces in out]
+        lanes = slice(128 * k, 128 * k + 128)
+        results = []
+        for i in targets:
+            starts = [i * plan.parents + p * plan.devices + first_block * plan.peers for p in range(plan.own)]
+            op_real = jnp.concatenate([a_real[a : a + many, lanes] for a in starts], 0)
+            op_imag = jnp.concatenate([a_imag[a : a + many, lanes] for a in starts], 0)
+            real = jnp.sum(op_real * out_real - op_imag * out_imag, 0, keepdims=True)
+            imag = jnp.sum(op_real * out_imag + op_imag * out_real, 0, keepdims=True)
+            results.append((i, real, imag))
+        return results
+
+    def kernel(self, table_in, received, a_real, a_imag, partial, table, tally, keys, lows):
+        plan = self.plan
         self.read(received, keys, lows)
         self.count(0, keys, lows, tally)
         self.fill(table_in, table)
         self.sum_operators(tally, table, a_real, a_imag)
+        for k in range(plan.tiles):
+            for i, real, imag in self.apply([received], 0, a_real, a_imag, range(self.group), k):
+                at = i * 2 * plan.tiles + k
+                partial[at : at + 1, :] = real
+                partial[at + plan.tiles : at + plan.tiles + 1, :] = imag
 
 
 def translate_kernel(plan, tallies, ready):
@@ -318,7 +346,7 @@
 
     def kernel(*refs):
         if ready:
-            a_real, a_imag, *refs = refs
+            a_real, a_imag, partial, *refs = refs
             blocks = refs[: plan.cores]
             (out,) = refs[plan.cores :]
         else:
@@ -328,33 +356,17 @@
             tallies.read(blocks[0], keys, lows)
             tallies.fill(table_in, table)
 
-        def pattern(part, k):
-            pieces = []
-            for p in range(plan.own):
-                if k < plan.full:
-                    row, turn = (2 * p + part) * plan.full + k, 0
-                else:
-                    row, turn = plan.rest_at(p, part)
-                for block in blocks:
-                    piece = block[pl.ds(row, plan.peers, stride=plan.rows), :]
-                    pieces.append(pltpu.roll(piece, 128 - turn, 1) if turn else piece)
-            return jnp.concatenate(pieces, 0)
-
         def do_group(first_target):
             if not ready:
                 tallies.count(first_target, keys, lows, tally)
                 tallies.sum_operators(tally, table, a_real, a_imag)
             for k in range(plan.tiles):
-                lanes = slice(128 * k, 128 * k + 128)
-                out_real = pattern(0, k)
-                out_imag = pattern(1, k)
-                for i in range(group):
-                    rows = slice(i * plan.parents, (i + 1) * plan.parents)
-                    op_real = a_real[rows, lanes]
-                    op_imag = a_imag[rows, lanes]
-                    real = jnp.sum(op_real * out_real - op_imag * out_imag, 0, keepdims=True)
-                    imag = jnp.sum(op_real * out_imag + op_imag * out_real, 0, keepdims=True)
+                start = 1 if ready else 0
+                for i, real, imag in tallies.apply(blocks[start:], start, a_real, a_imag, range(group), k):
                     at = (first_target + i) * 2 * plan.tiles + k
+                    if ready:
+                        real = real + partial[at : at + 1, :]
+                        imag = imag + partial[at + plan.tiles : at + plan.tiles + 1, :]
                     out[pl.ds(at, 1), :] = real
                     out[pl.ds(at + plan.tiles, 1), :] = imag
 
@@ -478,15 +490,15 @@
         blocks.append(lax.ppermute(received, "narrow", [(i, i ^ 1) for i in range(n_narrow)]))
 
     tallies = Tally(plan)
-    ready = tallies.targets == tallies.group
+    ready = tallies.targets == tallies.group and plan.cores > 1
     sums = jax.ShapeDtypeStruct((tallies.rows, plan.width), F32)
     scratch = [pltpu.VMEM((2, plan.width, tallies.shape[1]), BF16), pltpu.VMEM(tallies.shape, BF16)] + tallies.scratch
     if ready:
         operands = pl.pallas_call(
             tallies.kernel,
-            out_shape=(sums, sums),
+            out_shape=(sums, sums, jax.ShapeDtypeStruct((tallies.targets * 2 * plan.tiles, 128), F32)),
             in_specs=[vmem, vmem],
-            out_specs=(vmem, vmem),
+            out_specs=(vmem,) * 3,
             scratch_shapes=scratch,
             cost_estimate=pl.CostEstimate(flops=10**9, bytes_accessed=10**6, transcendentals=0),
             compiler_params=pltpu.CompilerParams(vmem_limit_bytes=16 * MIB),

time: 31.9 us -> 31.8 us (level)
  no operation moved by 1% of the time
where the time goes in v8:
time: 31.8 us; the launch traced here: 31.5 us
  blocking collectives  20.3 us (64%)
  Pallas kernels  10 us (31%)
  starting transfers between devices  1.14 us (4%)
    all_to_all x1, blocking collectives, on_device(): lax.all_to_all(send, ('wide', 'narrow'), split_axis=0, concat_axis=0, til...  12.6 us
    all_to_all x1, blocking collectives, on_device(): lax.all_to_all(incoming, ('wide', 'narrow'), split_axis=0, concat_axis=0,...  7.73 us
    pallas_call x1, Pallas kernels, on_device(): pl.pallas_call(upward_kernel(plan, cuts), out_shape=jax.ShapeDtypeStruct(...  4.91 us
    pallas_call x1, Pallas kernels, on_device(): pl.pallas_call(downward_kernel(plan), out_shape=jax.ShapeDtypeStruct((box...  2.76 us
    pallas_call x1, Pallas kernels, on_device(): pl.pallas_call(tallies.kernel, out_shape=(sums, sums, jax.ShapeDtypeStruc...  1.94 us
    ppermute x1, starting transfers between devices, on_device(): lax.ppermute(received, 'narrow', [(i, i ^ 1) for i in range(n_narrow)])  1.14 us
  transfers between devices with their start and end apart: 1, of which 0 were waited for; matrix products, arithmetic and copies ran while one was open for 0% of the time, Pallas kernels for 6%

profile of v8, /device:TPU:0, one launch (start us, length us, event | category | flops | bytes accessed | tf_op | source)
XLA Modules:
  0.0 31.5 jit_solution(15561151497682082082)
XLA Ops:
  0.0 0.0 copy-start.2
  0.0 0.0 slice-start
  0.0 4.9 %upward.1 = f32[240,128]{1,0:T(8,128)} custom-call(s32[2]{0:T(128)} %counts_hbm.1, bf16[16,2,512]{2,1,0:T(2,128)(2,1)} %coef_hbm.1, bf16[882,2,512]{2,1,0:T(2,128)(2,1)} %bitcast.8, bf16[882,3328]{1,0:T(8,128)(2,1)} %interp.1, f32[8,3328]{1,0:T(8,128)} %angles.1, s32[2,189]{1,0:T(2,128)} %sources_hbm.1, s32[2,189]{1,0:T(2,128)} %operators_hbm.1), custom_call_target="tpu_custom_call" | custom-call | tf_op jit(solution)/shard_map/upward/pallas_call | solution.py:458
  4.9 12.6 %all_to_all.10 = f32[16,1,1920]{2,1,0:T(1,128)S(1)} all-to-all(f32[16,1,1920]{2,1,0:T(1,128)} %bitcast.16), channel_id=1, replica_groups={{21,23,17,19,12,14,8,10,4,6,0,2,25,27,29,31},{20,22,16,18,13,15,9,11,5,..., dimensions={0} | all-to-all | bytes 245760 | tf_op jit(solution)/shard_map/all_to_all | solution.py:485
  17.5 1.1 %collective-permute-start = (f32[240,128]{1,0:T(8,128)S(1)}, f32[240,128]{1,0:T(8,128)S(1)}, u32[]{:S(2)}, u32[]{:S(2)}) collective-permute-start(f32[240,128]{1,0:T(8,128)S(1)} %bitcast.10), channel_id=1, source_target_pairs={{0,1},{1,0},{2,3},{3,2},{4,5},{5,4},{6,7},{7,6},{8,9},{9,8},{10,11... | collective-permute-start | bytes 368648 | tf_op jit(solution)/shard_map/ppermute | solution.py:490
  18.6 0.0 copy-done.2
  18.6 0.0 slice-start.1
  18.6 1.9 %operators.1 = (f32[1024,512]{1,0:T(8,128)S(1)}, f32[1024,512]{1,0:T(8,128)S(1)}, f32[128,128]{1,0:T(8,128)S(1)}) custom-call(f32[2,416,316]{2,1,0:T(8,128)S(1)} %bitcast.15, f32[240,128]{1,0:T(8,128)S(1)} %bitcast.11), custom_call_target="tpu_custom_call" | custom-call | flops 1000000000 | bytes 1000000 | tf_op jit(solution)/shard_map/operators/pallas_call | solution.py:497
  20.6 0.0 collective-permute-done.refs_4_
  20.6 0.0 copy-start
  20.6 0.0 copy-start.1
  20.6 0.4 %translate.1 = f32[128,128]{1,0:T(8,128)S(1)} custom-call(f32[1024,512]{1,0:T(8,128)S(1)} %get-tuple-element.8.refs_0_, f32[1024,512]{1,0:T(8,128)S(1)} %get-tuple-element.9.refs_1_, f32[128,128]{1,0:T(8,128)S(1)} %get-tuple-element.10.refs_2_, f32[240,128]{1,0:T(8,128)S(1)} %bitcast.12, f32[240,128]{1,0:T(8,128)S(1)} %collective-permute-done.refs_4_), custom_call_target="tpu_custom_call" | custom-call | tf_op jit(solution)/shard_map/translate/pallas_call | solution.py:512
  21.0 7.7 %all_to_all.11 = f32[8,16,128]{2,1,0:T(8,128)S(1)} all-to-all(f32[8,16,128]{2,1,0:T(8,128)S(1)} %bitcast.13), channel_id=1, replica_groups={{21,17,12,8,4,0,25,29},{20,16,13,9,5,1,24,28},{23,19,14,10,6,2,27,31},{..., dimensions={0} | all-to-all | bytes 131072 | tf_op jit(solution)/shard_map/all_to_all | solution.py:523
  28.7 0.0 slice-done
  28.7 0.0 slice-done.1
  28.8 0.0 copy-done
  28.8 0.0 copy-done.1
  28.8 2.8 %downward.1 = f32[16,2,512]{2,1,0:T(2,128)} custom-call(f32[128,128]{1,0:T(8,128)S(1)} %bitcast.14, f32[8,3328]{1,0:T(8,128)S(1)} %copy-done.1, bf16[882,3328]{1,0:T(8,128)(2,1)S(1)} %bitcast.7, bf16[882,2,512]{2,1,0:T(2,128)(2,1)S(1)} %bitcast.9), custom_call_target="tpu_custom_call" | custom-call | tf_op jit(solution)/shard_map/downward/pallas_call | solution.py:528
  (1 shorter events, 0.0 us)
Async XLA Ops:
  0.0 18.6 %copy-start.2 = (f32[316,2,416]{0,2,1:T(8,128)S(1)}, f32[316,2,416]{0,2,1:T(8,128)}, u32[]{:S(2)}) copy-start(f32[316,2,416]{0,2,1:T(8,128)} %param.12) | copy-start | bytes 3154948
  0.0 28.7 %slice-start = ((s8[5910528]{0:T(1024)(128)(4,1)}), s8[1716224]{0:T(1024)(128)(4,1)S(1)}, s32[]{:S(2)}) async-start(s8[5910528]{0:T(1024)(128)(4,1)} %bitcast.6), calls=%async_computation.2 | async-start | bytes 3432448
  17.5 3.1 %collective-permute-start = (f32[240,128]{1,0:T(8,128)S(1)}, f32[240,128]{1,0:T(8,128)S(1)}, u32[]{:S(2)}, u32[]{:S(2)}) collective-permute-start(f32[240,128]{1,0:T(8,128)S(1)} %bitcast.10), channel_id=1, source_target_pairs={{0,1},{1,0},{2,3},{3,2},{4,5},{5,4},{6,7},{7,6},{8,9},{9,8},{10,11... | collective-permute-start | bytes 368648 | tf_op jit(solution)/shard_map/ppermute | solution.py:490
  18.6 10.1 %slice-start.1 = ((s8[5910528]{0:T(1024)(128)(4,1)}), s8[4194304]{0:T(1024)(128)(4,1)S(1)}, s32[]{:S(2)}) async-start(s8[5910528]{0:T(1024)(128)(4,1)} %bitcast.6), calls=%async_computation.3 | async-start | bytes 8388608
  20.6 8.2 %copy-start = (bf16[2,512,882]{1,0,2:T(2,128)(2,1)S(1)}, bf16[2,512,882]{1,0,2:T(2,128)(2,1)}, u32[]{:S(2)}) copy-start(bf16[2,512,882]{1,0,2:T(2,128)(2,1)} %param.9) | copy-start | bytes 5419012
  20.6 8.2 %copy-start.1 = (f32[8,3328]{1,0:T(8,128)S(1)}, f32[8,3328]{1,0:T(8,128)}, u32[]{:S(2)}) copy-start(f32[8,3328]{1,0:T(8,128)} %angles.1) | copy-start | bytes 319492

commit v9 on v8

--- a/solution.py
+++ b/solution.py
@@ -19,7 +19,8 @@
         self.devices = n_wide * n_narrow
         self.parents = own * self.devices
         first = n_wide * 5 // 8
-        self.order = list(range(first, -1, -1)) + list(range(first + 1, n_wide))
+        self.order_back = list(range(first, -1, -1)) + list(range(first + 1, n_wide))
+        self.order = [first, first - 1, *range(first + 1, n_wide), *range(first - 2, -1, -1)]
         self.cores = 2 if n_narrow % 2 == 0 else 1
         self.pairs = n_narrow // self.cores
         self.peers = n_wide * self.pairs
@@ -61,7 +62,7 @@
 
     def wide_groups(self):
         return [
-            [self.device(w, pair, label) for w in self.order]
+            [self.device(w, pair, label) for w in self.order_back]
             for pair in range(self.pairs)
             for label in range(self.cores)
         ]
@@ -265,9 +266,9 @@
         for e in range(plan.list_rows):
             rows = [
                 received[
-                    pl.ds((own_block + i * plan.pairs) * plan.rows + plan.list_row + p * plan.list_rows + e, 1), :
+                    pl.ds((own_block + plan.order.index(w) * plan.pairs) * plan.rows + plan.list_row + p * plan.list_rows + e, 1), :
                 ]
-                for i in range(plan.n_wide)
+                for w in plan.order_back
                 for p in range(plan.own)
             ]
             words.append(jnp.concatenate(rows, 0).astype(jnp.int32))
@@ -388,7 +389,7 @@
         lane = lax.broadcasted_iota(jnp.int32, (parts, plan.width), 1)
         received[0 : arrived.shape[0], :] = arrived[...]
         inner[...] = jnp.zeros(inner.shape, F32)
-        for i, w in enumerate(plan.order):
+        for i, w in enumerate(plan.order_back):
             base = plan.dirs * w // 128 * 128
             shift = plan.dirs * w % 128
             span = -(-(shift + plan.dirs) // 128) * 128

time: 31.8 us -> 31.9 us (level)
  no operation moved by 1% of the time
where the time goes in v9:
time: 31.9 us; the launch traced here: 31.6 us
  blocking collectives  20.2 us (63%)
  Pallas kernels  10 us (31%)
  starting transfers between devices  1.21 us (4%)
    all_to_all x1, blocking collectives, on_device(): lax.all_to_all(send, ('wide', 'narrow'), split_axis=0, concat_axis=0, til...  12.3 us
    all_to_all x1, blocking collectives, on_device(): lax.all_to_all(incoming, ('wide', 'narrow'), split_axis=0, concat_axis=0,...  7.93 us
    pallas_call x1, Pallas kernels, on_device(): pl.pallas_call(upward_kernel(plan, cuts), out_shape=jax.ShapeDtypeStruct(...  4.91 us
    pallas_call x1, Pallas kernels, on_device(): pl.pallas_call(downward_kernel(plan), out_shape=jax.ShapeDtypeStruct((box...  2.77 us
    pallas_call x1, Pallas kernels, on_device(): pl.pallas_call(tallies.kernel, out_shape=(sums, sums, jax.ShapeDtypeStruc...  1.94 us
    ppermute x1, starting transfers between devices, on_device(): lax.ppermute(received, 'narrow', [(i, i ^ 1) for i in range(n_narrow)])  1.21 us
  transfers between devices with their start and end apart: 1, of which 0 were waited for; matrix products, arithmetic and copies ran while one was open for 0% of the time, Pallas kernels for 6%

profile of v9, /device:TPU:0, one launch (start us, length us, event | category | flops | bytes accessed | tf_op | source)
XLA Modules:
  0.0 31.6 jit_solution(13852031481482940748)
XLA Ops:
  0.0 0.0 copy-start.2
  0.0 0.0 slice-start
  0.0 4.9 %upward.1 = f32[240,128]{1,0:T(8,128)} custom-call(s32[2]{0:T(128)} %counts_hbm.1, bf16[16,2,512]{2,1,0:T(2,128)(2,1)} %coef_hbm.1, bf16[882,2,512]{2,1,0:T(2,128)(2,1)} %bitcast.8, bf16[882,3328]{1,0:T(8,128)(2,1)} %interp.1, f32[8,3328]{1,0:T(8,128)} %angles.1, s32[2,189]{1,0:T(2,128)} %sources_hbm.1, s32[2,189]{1,0:T(2,128)} %operators_hbm.1), custom_call_target="tpu_custom_call" | custom-call | tf_op jit(solution)/shard_map/upward/pallas_call | solution.py:459
  4.9 12.3 %all_to_all.10 = f32[16,1,1920]{2,1,0:T(1,128)S(1)} all-to-all(f32[16,1,1920]{2,1,0:T(1,128)} %bitcast.16), channel_id=1, replica_groups={{21,23,17,19,25,27,29,31,12,14,8,10,4,6,0,2},{20,22,16,18,24,26,28,30,1..., dimensions={0} | all-to-all | bytes 245760 | tf_op jit(solution)/shard_map/all_to_all | solution.py:486
  17.2 1.2 %collective-permute-start = (f32[240,128]{1,0:T(8,128)S(1)}, f32[240,128]{1,0:T(8,128)S(1)}, u32[]{:S(2)}, u32[]{:S(2)}) collective-permute-start(f32[240,128]{1,0:T(8,128)S(1)} %bitcast.10), channel_id=1, source_target_pairs={{0,1},{1,0},{2,3},{3,2},{4,5},{5,4},{6,7},{7,6},{8,9},{9,8},{10,11... | collective-permute-start | bytes 368648 | tf_op jit(solution)/shard_map/ppermute | solution.py:491
  18.5 0.0 copy-done.2
  18.5 0.0 slice-start.1
  18.5 1.9 %operators.1 = (f32[1024,512]{1,0:T(8,128)S(1)}, f32[1024,512]{1,0:T(8,128)S(1)}, f32[128,128]{1,0:T(8,128)S(1)}) custom-call(f32[2,416,316]{2,1,0:T(8,128)S(1)} %bitcast.15, f32[240,128]{1,0:T(8,128)S(1)} %bitcast.11), custom_call_target="tpu_custom_call" | custom-call | flops 1000000000 | bytes 1000000 | tf_op jit(solution)/shard_map/operators/pallas_call | solution.py:498
  20.4 0.0 collective-permute-done.refs_4_
  20.4 0.0 copy-start
  20.4 0.0 copy-start.1
  20.4 0.4 %translate.1 = f32[128,128]{1,0:T(8,128)S(1)} custom-call(f32[1024,512]{1,0:T(8,128)S(1)} %get-tuple-element.8.refs_0_, f32[1024,512]{1,0:T(8,128)S(1)} %get-tuple-element.9.refs_1_, f32[128,128]{1,0:T(8,128)S(1)} %get-tuple-element.10.refs_2_, f32[240,128]{1,0:T(8,128)S(1)} %bitcast.12, f32[240,128]{1,0:T(8,128)S(1)} %collective-permute-done.refs_4_), custom_call_target="tpu_custom_call" | custom-call | tf_op jit(solution)/shard_map/translate/pallas_call | solution.py:513
  20.8 7.9 %all_to_all.11 = f32[8,16,128]{2,1,0:T(8,128)S(1)} all-to-all(f32[8,16,128]{2,1,0:T(8,128)S(1)} %bitcast.13), channel_id=1, replica_groups={{21,17,12,8,4,0,25,29},{20,16,13,9,5,1,24,28},{23,19,14,10,6,2,27,31},{..., dimensions={0} | all-to-all | bytes 131072 | tf_op jit(solution)/shard_map/all_to_all | solution.py:524
  28.8 0.0 slice-done
  28.8 0.0 slice-done.1
  28.8 0.0 copy-done
  28.8 0.0 copy-done.1
  28.8 2.8 %downward.1 = f32[16,2,512]{2,1,0:T(2,128)} custom-call(f32[128,128]{1,0:T(8,128)S(1)} %bitcast.14, f32[8,3328]{1,0:T(8,128)S(1)} %copy-done.1, bf16[882,3328]{1,0:T(8,128)(2,1)S(1)} %bitcast.7, bf16[882,2,512]{2,1,0:T(2,128)(2,1)S(1)} %bitcast.9), custom_call_target="tpu_custom_call" | custom-call | tf_op jit(solution)/shard_map/downward/pallas_call | solution.py:529
  (1 shorter events, 0.0 us)
Async XLA Ops:
  0.0 18.5 %copy-start.2 = (f32[316,2,416]{0,2,1:T(8,128)S(1)}, f32[316,2,416]{0,2,1:T(8,128)}, u32[]{:S(2)}) copy-start(f32[316,2,416]{0,2,1:T(8,128)} %param.12) | copy-start | bytes 3154948
  0.0 28.8 %slice-start = ((s8[5910528]{0:T(1024)(128)(4,1)}), s8[1716224]{0:T(1024)(128)(4,1)S(1)}, s32[]{:S(2)}) async-start(s8[5910528]{0:T(1024)(128)(4,1)} %bitcast.6), calls=%async_computation.2 | async-start | bytes 3432448
  17.2 3.2 %collective-permute-start = (f32[240,128]{1,0:T(8,128)S(1)}, f32[240,128]{1,0:T(8,128)S(1)}, u32[]{:S(2)}, u32[]{:S(2)}) collective-permute-start(f32[240,128]{1,0:T(8,128)S(1)} %bitcast.10), channel_id=1, source_target_pairs={{0,1},{1,0},{2,3},{3,2},{4,5},{5,4},{6,7},{7,6},{8,9},{9,8},{10,11... | collective-permute-start | bytes 368648 | tf_op jit(solution)/shard_map/ppermute | solution.py:491
  18.5 10.3 %slice-start.1 = ((s8[5910528]{0:T(1024)(128)(4,1)}), s8[4194304]{0:T(1024)(128)(4,1)S(1)}, s32[]{:S(2)}) async-start(s8[5910528]{0:T(1024)(128)(4,1)} %bitcast.6), calls=%async_computation.3 | async-start | bytes 8388608
  20.4 8.4 %copy-start = (bf16[2,512,882]{1,0,2:T(2,128)(2,1)S(1)}, bf16[2,512,882]{1,0,2:T(2,128)(2,1)}, u32[]{:S(2)}) copy-start(bf16[2,512,882]{1,0,2:T(2,128)(2,1)} %param.9) | copy-start | bytes 5419012
  20.4 8.4 %copy-start.1 = (f32[8,3328]{1,0:T(8,128)S(1)}, f32[8,3328]{1,0:T(8,128)}, u32[]{:S(2)}) copy-start(f32[8,3328]{1,0:T(8,128)} %angles.1) | copy-start | bytes 319492
